TPU v7x, 512 devices: a whole 4x4x16 slice. The times are simulated.
512 devices in a mesh: space: 128 (over z, y, core), code: 4 (over x).
Axes of the slice: x: 4, y: 4, z: 16, core: 2. Of those that a mesh axis runs over, the one named last changes fastest.
Arguments:
- geometry: bfloat16 [4, 6, 1048576], P('code', None, 'space'), as said below
- codebook: bfloat16 [48, 4096], P(None, 'code'), may hold values from -3 to 3
- word_ids: int32 [1048576], P('space'), may hold values from 0 to 4095
- residual: bfloat16 [12, 1048576], P(None, 'space'), may hold values from -2 to 2
- send_list: int32 [4, 128, 128], P('code', 'space'), may hold values from 0 to 63
- tile_list: int32 [4, 1024, 4], P('code', 'space'), may hold values from 0 to 127, as said below
- rays: float32 [4, 3, 262144], P('code', None, 'space'), as said below
- target: int32 [4, 3, 262144], P('code', None, 'space'), may hold values from 0 to 255
Outputs:
- rendered: float32 [4, 3, 262144], P('code', None, 'space')
- foot_grad: float32 [4, 6, 1048576], P('code', None, 'space')
- resid_grad: float32 [12, 1048576], P(None, 'space')
- code_grad: float32 [48, 4096], P(None, 'code')
Inputs may be any that keep to these rules, and one draw needn't show every extreme that they name: `tile_list`: each row names 4 different owners. `geometry`: conics are positive definite, |b| at most 0.6 sqrt(a c); opacities are positive and at most 0.5. `rays`: every ray has length 0.8 to 1.2; directions may point anywhere.
All inputs are finite; a program needn't handle non-finite values.
Results may differ from a plain program's by a relative error of at most 0.0021.
Values may be sent and summed in bfloat16 or wider, within the bound.
A program may use at most 64 MiB of HBM per device.

v0:
```python
import math

import jax
import jax.numpy as jnp
from jax import lax
from jax.sharding import PartitionSpec as P

WORDS = 4096
COEF = 48
RESID = 12
GEO = 6
BLOCK = 128
LIST = 4
SIDE = 16
TILE_PIX = 256


band_zero = 0.28209479177387814
band_one = 0.4886025119029199
band_two = (
    1.0925484305920792,
    -1.0925484305920792,
    0.31539156525252005,
    -1.0925484305920792,
    0.5462742152960396,
)
band_three = (
    -0.5900435899266435,
    2.890611442640554,
    -0.4570457994644658,
    0.3731763325901154,
    -0.4570457994644658,
    1.445305721320277,
    -0.5900435899266435,
)


def harmonics(direction):
    length = jnp.sqrt(jnp.sum(direction * direction, axis=0))
    coord_x = direction[0] / length
    coord_y = direction[1] / length
    coord_z = direction[2] / length
    square_x = coord_x * coord_x
    square_y = coord_y * coord_y
    square_z = coord_z * coord_z
    entries = [
        band_zero * jnp.ones_like(coord_x),
        -band_one * coord_y,
        band_one * coord_z,
        -band_one * coord_x,
        band_two[0] * coord_x * coord_y,
        band_two[1] * coord_y * coord_z,
        band_two[2] * (2.0 * square_z - square_x - square_y),
        band_two[3] * coord_x * coord_z,
        band_two[4] * (square_x - square_y),
        band_three[0] * coord_y * (3.0 * square_x - square_y),
        band_three[1] * coord_x * coord_y * coord_z,
        band_three[2] * coord_y * (4.0 * square_z - square_x - square_y),
        band_three[3] * coord_z * (2.0 * square_z - 3.0 * square_x - 3.0 * square_y),
        band_three[4] * coord_x * (4.0 * square_z - square_x - square_y),
        band_three[5] * coord_z * (square_x - square_y),
        band_three[6] * coord_x * (square_x - 3.0 * square_y),
    ]
    return jnp.stack(entries)


def pixel_offsets(side):
    pixel_index = jnp.arange(side * side, dtype=jnp.int32)
    offset_u = (pixel_index % side).astype(jnp.float32) - (side - 1) * 0.5
    offset_v = (pixel_index // side).astype(jnp.float32) - (side - 1) * 0.5
    return jnp.stack([offset_u, offset_v])


def composite(footprint, palette, harmonic_rows, offsets):
    delta_u = offsets[0][:, None] - footprint[0][None, :]
    delta_v = offsets[1][:, None] - footprint[1][None, :]
    exponent = -0.5 * (
        footprint[2] * delta_u * delta_u
        + 2.0 * footprint[3] * delta_u * delta_v
        + footprint[4] * delta_v * delta_v
    )
    absorb = footprint[5] * jnp.exp(exponent)
    keep_log = jnp.log1p(-absorb)
    before = jnp.cumsum(keep_log, axis=1) - keep_log
    weight = jnp.exp(before) * absorb
    mixed = jnp.dot(weight, palette.T, precision=lax.Precision.HIGHEST)
    mixed = mixed.reshape(mixed.shape[0], 16, 3)
    return (
        jnp.einsum("kp,pkc->cp", harmonic_rows, mixed, precision=lax.Precision.HIGHEST)
        + 0.5 * jnp.sum(weight, axis=1)[None, :]
    )


def render_group(footprint, palette, harmonic_rows, destination_group, offsets):

    def forward(foot_all, palette_group):
        return jax.vmap(composite, in_axes=(0, 0, 0, None))(
            foot_all, palette_group, harmonic_rows, offsets
        )

    images, pullback = jax.vjp(forward, footprint, palette)
    grad_foot, grad_palette = pullback(images - destination_group)
    return (images, grad_foot, grad_palette)


def decode(codebook, word_ids, residual):
    looked = jnp.take(codebook, word_ids, axis=1).astype(jnp.float32)
    upper = looked[:RESID] + residual.astype(jnp.float32)
    decoded = jnp.concatenate([upper, looked[RESID:]], axis=0).astype(jnp.bfloat16)
    return lax.optimization_barrier(decoded)


def on_device(geometry, codebook, word_ids, residual, send_list, tile_list, rays, target):
    n_space = lax.axis_size("space")
    blocks = word_ids.shape[0] // BLOCK
    tiles_here = tile_list.shape[1]
    list_width = LIST * BLOCK
    full_book = lax.all_gather(codebook, "code", axis=1, tiled=True)
    sent_blocks = send_list[0, 0]
    foot_out = jnp.take(geometry[0].reshape(GEO, blocks, BLOCK), sent_blocks, axis=1)
    decoded = decode(full_book, word_ids, residual)
    palette_out = jnp.take(decoded.reshape(COEF, blocks, BLOCK), sent_blocks, axis=1)
    foot_in, palette_in = (
        lax.all_to_all(foot_out, "space", split_axis=1, concat_axis=1, tiled=True),
        lax.all_to_all(palette_out, "space", split_axis=1, concat_axis=1, tiled=True),
    )
    tile_rows = tile_list[0]
    flat_rows = tile_rows.reshape(-1)
    foot_tiles = (
        jnp.take(foot_in, flat_rows, axis=1).reshape(GEO, tiles_here, list_width).transpose(1, 0, 2)
    )
    palette_tiles = (
        jnp.take(palette_in, flat_rows, axis=1)
        .reshape(COEF, tiles_here, list_width)
        .transpose(1, 0, 2)
    )
    harmonic_tiles = harmonics(rays[0]).reshape(16, tiles_here, TILE_PIX).transpose(1, 0, 2)
    target_tiles = (
        (target[0].astype(jnp.float32) / 255.0).reshape(3, tiles_here, TILE_PIX).transpose(1, 0, 2)
    )
    per_step = math.gcd(tiles_here, 2)
    step_count = tiles_here // per_step
    offsets = pixel_offsets(SIDE)

    def render_step(inputs):
        foot_group, palette_group, harmonic_group, destination_group = inputs
        return render_group(
            foot_group.astype(jnp.float32),
            palette_group.astype(jnp.float32),
            harmonic_group,
            destination_group,
            offsets,
        )

    images, grad_foot, grad_palette = lax.map(
        render_step,
        (
            foot_tiles.reshape(step_count, per_step, GEO, list_width),
            palette_tiles.reshape(step_count, per_step, COEF, list_width),
            harmonic_tiles.reshape(step_count, per_step, 16, TILE_PIX),
            target_tiles.reshape(step_count, per_step, 3, TILE_PIX),
        ),
    )
    tile_grads = jnp.concatenate(
        [
            grad_foot.reshape(tiles_here, GEO, list_width),
            grad_palette.reshape(tiles_here, COEF, list_width),
        ],
        axis=1,
    )
    tile_grads = tile_grads.reshape(tiles_here, GEO + COEF, LIST, BLOCK)
    slot_hot = (
        tile_rows[:, :, None] == jnp.arange(n_space, dtype=jnp.int32)[None, None, :]
    ).astype(jnp.float32)
    slot_grads = jnp.einsum("tln,tclk->cnk", slot_hot, tile_grads, precision=lax.Precision.HIGHEST)
    sent_hot = (sent_blocks[:, None] == jnp.arange(blocks, dtype=jnp.int32)[None, :]).astype(
        jnp.float32
    )
    returned = lax.all_to_all(slot_grads, "space", split_axis=1, concat_axis=1, tiled=True)
    owned = jnp.einsum("cnk,nb->cbk", returned, sent_hot, precision=lax.Precision.HIGHEST).reshape(
        GEO + COEF, blocks * BLOCK
    )
    palette_owned = owned[GEO:]
    word_term = jax.ops.segment_sum(palette_owned.T, word_ids, num_segments=WORDS).T
    resid_part = palette_owned[:RESID]
    foot_grad = owned[:GEO]
    resid_grad = lax.psum(resid_part, "code")
    codeword_portion = lax.psum_scatter(word_term, "code", scatter_dimension=1, tiled=True)
    code_grad = lax.psum(codeword_portion, "space")
    rendered = (
        images.reshape(tiles_here, 3, TILE_PIX)
        .transpose(1, 0, 2)
        .reshape(1, 3, tiles_here * TILE_PIX)
    )
    return (rendered, foot_grad[None], resid_grad, code_grad)


def solution(mesh):
    placed = (
        P("code", None, "space"),
        P(None, "code"),
        P("space"),
        P(None, "space"),
        P("code", "space", None),
        P("code", "space", None),
        P("code", None, "space"),
        P("code", None, "space"),
    )
    return jax.shard_map(
        on_device,
        mesh=mesh,
        in_specs=placed,
        out_specs=(
            P("code", None, "space"),
            P("code", None, "space"),
            P(None, "space"),
            P(None, "code"),
        ),
        check_vma=False,
    )
```

profile of v0, /device:TPU:1, one launch (start us, length us, event | category | flops | bytes accessed | tf_op | source)
XLA Modules:
  0.0 949.4 jit_solution(1836377726024788179)
XLA Ops:
  10.2 20.6 %all-to-all-start = ((bf16[6,128,128]{2,0,1:T(8,128)(2,1)}), bf16[6,128,128]{2,0,1:T(8,128)(2,1)S(1)}, u32[]{:S(2)}, u32[]{:S(2)}) async-start(bf16[6,128,128]{2,0,1:T(8,128)(2,1)} %select_bitcast_fusion.3), calls=%async_computation | async-start | bytes 524288 | tf_op jit(solution)/shard_map/all_to_all | solution.py:124
  33.9 13.4 %all_gather.3 = bf16[48,4096]{0,1:T(8,128)(2,1)S(1)} all-gather(bf16[48,1024]{0,1:T(8,128)(2,1)S(1)} %copy.230), channel_id=1, replica_groups=mesh['space'=128,'code'=4] {'code'}, dimensions={1}, use_global_device_ids=true | all-gather | bytes 491520 | tf_op jit(solution)/shard_map/all_gather | solution.py:118
  47.4 27.9 %gather_fusion.2 = bf16[8192,48]{1,0:T(8,128)(2,1)S(1)} fusion(bf16[48,4096]{0,1:T(8,128)(2,1)S(1)} %all_gather.3, s32[8192]{0:T(1024)} %fusion.63), kind=kCustom, calls=%fused_computation.2 | custom fusion | bytes 1605632 | tf_op jit(solution)/shard_map/jit(_take)/gather | solution.py:107
  79.8 17.7 %all-to-all-start.1 = ((bf16[48,128,128]{2,0,1:T(8,128)(2,1)}), bf16[48,128,128]{2,0,1:T(8,128)(2,1)S(1)}, u32[]{:S(2)}, u32[]{:S(2)}) async-start(bf16[48,128,128]{2,0,1:T(8,128)(2,1)} %select_bitcast_fusion), calls=%async_computation.1 | async-start | bytes 3145728 | tf_op jit(solution)/shard_map/all_to_all | solution.py:125
  100.8 70.4 %all-to-all-done.1 = bf16[48,128,128]{2,0,1:T(8,128)(2,1)S(1)} async-done(((bf16[48,128,128]{2,0,1:T(8,128)(2,1)}), bf16[48,128,128]{2,0,1:T(8,128)(2,1)S(1)}, u32[]{:S(2)}, u32[]{:S(2)}) %all-to-all-start.1) | async-done | bytes 1572896 | tf_op jit(solution)/shard_map/all_to_all | solution.py:125
  173.1 107.2 %while.16 = (s32[]{:T(128)}, f32[4,2,3,256]{3,1,0,2:T(2,128)S(1)}, f32[4,2,6,512]{3,2,1,0:T(8,128)}, f32[4,2,48,512]{3,2,1,0:T(8,128)}, bf16[4,2,6,512]{3,1,0,2:...) while((s32[]{:T(128)}, f32[4,2,3,256]{3,1,0,2:T(2,128)S(1)}, ...), condition=%wide.region_14.15_spmd.clone.clone, body=%wide.region_1.14_spmd.clone.clone.sunk | while | flops 552732160 | bytes 30296212 | solution.py:155
  185.6 3.5 multiply_multiply_fusion.3
  190.1 4.3 fusion.96
  195.7 3.5 fusion.97
  212.4 3.5 multiply_multiply_fusion.3
  216.9 4.3 fusion.96
  222.4 3.5 fusion.97
  239.2 3.5 multiply_multiply_fusion.3
  243.6 4.3 fusion.96
  249.2 3.5 fusion.97
  266.0 3.5 multiply_multiply_fusion.3
  270.4 4.3 fusion.96
  282.6 4.8 convolution_bitcast_fusion.1
  287.3 4.5 copy.243
  291.9 173.2 %all_to_all.15 = f32[54,128,128]{2,0,1:T(8,128)S(1)} all-to-all(f32[54,128,128]{2,0,1:T(8,128)} %copy.243), channel_id=1, replica_groups=mesh['space'=128,'code'=4] {'space'}, dimensions={1} | all-to-all | bytes 7077888 | tf_op jit(solution)/shard_map/all_to_all | solution.py:179
  469.6 45.7 %scatter_custom_fusion = f32[4096,48]{1,0:T(8,128)} fusion(s32[8192]{0:T(1024)} %param.12, f32[8192,48]{1,0:T(8,128)} %bitcast.185, f32[]{:T(128)} %constant.114.clone.1), kind=kCustom, calls=%fused_computation.109 | custom fusion | flops 393216 | bytes 786944 | tf_op jit(solution)/shard_map/scatter-add | solution.py:184
  515.4 34.8 %reduce-scatter.2.cloned.1.call-done = f32[48,1024]{0,1:T(8,128)} async-done(((f32[48,4096]{0,1:T(8,128)}), f32[48,1024]{0,1:T(8,128)}) %reduce-scatter.2.cloned.1.call-update) | async-done | bytes 196624 | tf_op jit(solution)/shard_map/reduce_scatter | solution.py:188
  552.8 331.3 %all-reduce.11.cloned.1.call-done = f32[48,1024]{0,1:T(8,128)} async-done(((f32[48,1024]{0,1:T(8,128)}), f32[48,1024]{0,1:T(8,128)}) %all-reduce.11.cloned.1.call-update) | async-done | bytes 196624 | tf_op jit(solution)/shard_map/psum | solution.py:189
  886.0 54.9 %all-reduce.9.cloned.1.call-done = f32[12,8192]{1,0:T(8,128)} async-done(((f32[12,8192]{1,0:T(8,128)}), f32[12,8192]{1,0:T(8,128)}) %all-reduce.9.cloned.1.call-update) | async-done | bytes 393232 | tf_op jit(solution)/shard_map/psum | solution.py:187
  (305 shorter events, 93.3 us)
Async XLA Ops:
  7.2 1.4 copy-start
  10.2 69.6 %all-to-all-start = ((bf16[6,128,128]{2,0,1:T(8,128)(2,1)}), bf16[6,128,128]{2,0,1:T(8,128)(2,1)S(1)}, u32[]{:S(2)}, u32[]{:S(2)}) async-start(bf16[6,128,128]{2,0,1:T(8,128)(2,1)} %select_bitcast_fusion.3), calls=%async_computation | async-start | bytes 524288 | tf_op jit(solution)/shard_map/all_to_all | solution.py:124
  76.1 1.0 copy-start.2
  79.7 17.8 %copy-start.6 = (s32[1,8,4]{1,2,0:T(4,128)S(1)}, s32[1,8,4]{1,2,0:T(4,128)}, u32[]{:S(2)}) copy-start(s32[1,8,4]{1,2,0:T(4,128)} %param.15) | copy-start | bytes 388
  79.7 18.1 %copy-start.3 = (f32[1,3,2048]{2,0,1:T(1,128)S(1)}, f32[1,3,2048]{2,0,1:T(1,128)}, u32[]{:S(2)}) copy-start(f32[1,3,2048]{2,0,1:T(1,128)} %param.16) | copy-start | bytes 73732
  79.7 18.3 %copy-start.4 = (s32[1,3,2048]{2,0,1:T(1,128)S(1)}, s32[1,3,2048]{2,0,1:T(1,128)}, u32[]{:S(2)}) copy-start(s32[1,3,2048]{2,0,1:T(1,128)} %param.17) | copy-start | bytes 73732
  79.8 19.2 %copy-start.1 = (bf16[6,128,128]{2,0,1:T(8,128)(2,1)}, bf16[6,128,128]{2,0,1:T(8,128)(2,1)S(1)}, u32[]{:S(2)}) copy-start(bf16[6,128,128]{2,0,1:T(8,128)(2,1)S(1)} %all-to-all-done) | copy-start | bytes 589828
  79.8 91.4 %all-to-all-start.1 = ((bf16[48,128,128]{2,0,1:T(8,128)(2,1)}), bf16[48,128,128]{2,0,1:T(8,128)(2,1)S(1)}, u32[]{:S(2)}, u32[]{:S(2)}) async-start(bf16[48,128,128]{2,0,1:T(8,128)(2,1)} %select_bitcast_fusion), calls=%async_computation.1 | async-start | bytes 3145728 | tf_op jit(solution)/shard_map/all_to_all | solution.py:125
  97.5 452.7 %reduce-scatter.2.cloned.1.call-start = ((), (), s32[]{:S(2)}) async-start(), calls=%async_computation.5 | async-start | bytes 2621440 | tf_op jit(solution)/shard_map/reduce_scatter | solution.py:188
  100.7 72.4 %copy-start.5 = (f32[4,2,3,256]{3,1,0,2:T(2,128)S(1)}, f32[4,2,3,256]{3,1,0,2:T(2,128)}, u32[]{:S(2)}) copy-start(f32[4,2,3,256]{3,1,0,2:T(2,128)} %custom-call.11) | copy-start | bytes 73732
  291.9 173.2 %copy-start.7 = (s32[1,1,128]{2,1,0:T(1,128)S(1)}, s32[1,1,128]{2,1,0:T(1,128)}, u32[]{:S(2)}) copy-start(s32[1,1,128]{2,1,0:T(1,128)} %param.14) | copy-start | bytes 1540
  515.4 368.8 %all-reduce.11.cloned.1.call-start = ((), (), s32[]{:S(2)}) async-start(), calls=%async_computation.6 | async-start | bytes 1048576 | tf_op jit(solution)/shard_map/psum | solution.py:189
  550.2 390.7 %all-reduce.9.cloned.1.call-start = ((), (), s32[]{:S(2)}) async-start(), calls=%async_computation.4 | async-start | bytes 1048576 | tf_op jit(solution)/shard_map/psum | solution.py:187
Sparse Core Ops, SparseCore 0:
  515.5 34.6 reduce-scatter.1
  554.1 330.0 all-reduce.10
  887.1 53.8 all-reduce.8
where the time goes:
time: 952 us; the launch traced here: 949 us
  waiting for transfers between devices  491 us (52%)
  blocking collectives  187 us (20%)
  other arithmetic  108 us (11%)
  local copies, waits for them, and re-layouts  69 us (7%)
  matrix products  40.4 us (4%)
  starting transfers between devices  38.4 us (4%)
  between operations  14.2 us (1%)
    psum x1, waiting for transfers between devices, on_device(): code_grad = lax.psum(codeword_portion, 'space')  331 us
    all_to_all x1, blocking collectives, on_device(): lax.all_to_all(slot_grads, 'space', split_axis=1, concat_axis=1, tiled=True)  173 us
    all_to_all x1, waiting for transfers between devices, on_device(): lax.all_to_all(palette_out, 'space', split_axis=1, concat_axis=1, tiled=T...  70.4 us
    psum x1, waiting for transfers between devices, on_device(): resid_grad = lax.psum(resid_part, 'code')  54.9 us
    scatter-add x1, other arithmetic, on_device(): jax.ops.segment_sum(palette_owned.T, word_ids, num_segments=WORDS)  45.7 us
    reduce_scatter x1, waiting for transfers between devices, on_device(): lax.psum_scatter(word_term, 'code', scatter_dimension=1, tiled=True)  34.8 us
    dot_general x12, matrix products, composite(): mixed = jnp.dot(weight, palette.T, precision=lax.Precision.HIGHEST)  33.9 us
    gather x2, local copies, waits for them, and re-layouts, decode(): looked = jnp.take(codebook, word_ids, axis=1).astype(jnp.float32)  28.8 us
  transfers between devices with their start and end apart: 5, of which 4 were waited for; matrix products, arithmetic and copies ran while one was open for 4% of the time, Pallas kernels for 0%

commit v1 on v0

v1 whole, which is shorter than its diff:
```python
import functools
import math

import jax
import jax.numpy as jnp
import numpy as np
from jax import lax
from jax.experimental import pallas as pl
from jax.experimental.pallas import tpu as pltpu
from jax.sharding import PartitionSpec as P

WORDS = 4096
COEF = 48
RESID = 12
GEO = 6
BLOCK = 128
LIST = 4
SIDE = 16
TILE_PIX = 256
WIDTH = LIST * BLOCK
GROUPS = 4
GWORDS = WORDS // GROUPS
ROWS_OUT = 24
ROWS_BACK = 32
LOG2E = 1.4426950408889634
F32 = jnp.float32
BF16 = jnp.bfloat16

band_zero = 0.28209479177387814
band_one = 0.4886025119029199
band_two = (
    1.0925484305920792,
    -1.0925484305920792,
    0.31539156525252005,
    -1.0925484305920792,
    0.5462742152960396,
)
band_three = (
    -0.5900435899266435,
    2.890611442640554,
    -0.4570457994644658,
    0.3731763325901154,
    -0.4570457994644658,
    1.445305721320277,
    -0.5900435899266435,
)


def harmonic_rows(ray_x, ray_y, ray_z):
    length = jnp.sqrt(ray_x * ray_x + ray_y * ray_y + ray_z * ray_z)
    x = ray_x / length
    y = ray_y / length
    z = ray_z / length
    xx, yy, zz = x * x, y * y, z * z
    return [
        band_zero * jnp.ones_like(x),
        -band_one * y,
        band_one * z,
        -band_one * x,
        band_two[0] * x * y,
        band_two[1] * y * z,
        band_two[2] * (2.0 * zz - xx - yy),
        band_two[3] * x * z,
        band_two[4] * (xx - yy),
        band_three[0] * y * (3.0 * xx - yy),
        band_three[1] * x * y * z,
        band_three[2] * y * (4.0 * zz - xx - yy),
        band_three[3] * z * (2.0 * zz - 3.0 * xx - 3.0 * yy),
        band_three[4] * x * (4.0 * zz - xx - yy),
        band_three[5] * z * (xx - yy),
        band_three[6] * x * (xx - 3.0 * yy),
    ]


def nn(a, b):
    return lax.dot_general(a, b, (((1,), (0,)), ((), ())), preferred_element_type=F32)


def nt(a, b):
    return lax.dot_general(a, b, (((1,), (1,)), ((), ())), preferred_element_type=F32)


def tn(a, b):
    return lax.dot_general(a, b, (((0,), (0,)), ((), ())), preferred_element_type=F32)


def pack_kernel(send_ref, geo_ref, word_ref, resid_ref, out_ref, blocks_ref):
    blocks = blocks_ref.shape[0]

    def build(b, carry):
        lanes = pl.ds(pl.multiple_of(b * BLOCK, BLOCK), BLOCK)
        ids = word_ref[pl.ds(b, 1), :]
        high = (ids >> 8).astype(F32)
        low = (ids & 255).astype(F32)
        geo = geo_ref[:, lanes].astype(F32)
        resid = resid_ref[:, lanes].astype(F32)
        whole = jnp.concatenate([geo, high, low, resid, jnp.zeros((4, BLOCK), F32)], axis=0)
        blocks_ref[b] = whole.astype(BF16)
        return carry

    lax.fori_loop(0, blocks, build, 0, unroll=4)

    def copy(d, carry):
        out_ref[d] = blocks_ref[send_ref[d]]
        return carry

    lax.fori_loop(0, out_ref.shape[0], copy, 0, unroll=8)


def pack(sent, geo, words, resid):
    blocks = words.shape[0]
    return pl.pallas_call(
        pack_kernel,
        out_shape=jax.ShapeDtypeStruct((sent.shape[0], ROWS_OUT, BLOCK), BF16),
        in_specs=[pl.BlockSpec(memory_space=pltpu.SMEM)]
        + [pl.BlockSpec(memory_space=pltpu.VMEM)] * 3,
        out_specs=pl.BlockSpec(memory_space=pltpu.VMEM),
        scratch_shapes=[pltpu.VMEM((blocks, ROWS_OUT, BLOCK), BF16)],
        name="pack",
    )(sent, geo, words, resid)


def constants():
    perm = np.zeros((56, 56), np.float32)
    for j in range(16):
        for ch in range(3):
            perm[ch * 16 + j, 3 * j + ch] = 1.0
    perm[48, 48] = 1.0
    spread = np.zeros((256, 56), np.float32)
    for j in range(16):
        for g in range(GROUPS):
            for ch in range(3):
                spread[j * 16 + g * 3 + ch, ch * 16 + j] = 1.0
    return jnp.asarray(perm, BF16), jnp.asarray(spread, BF16)


def render_kernel(
    tile_ref,
    recv_ref,
    book_ref,
    rays_ref,
    target_ref,
    perm_ref,
    spread_ref,
    img_ref,
    back_ref,
    acc_ref,
    words_ref,
    harm_ref,
    tri_ref,
    tris_ref,
    hot_ref,
    e_ref,
    log_ref,
    cum_ref,
    wp_ref,
    wb_ref,
    wl_ref,
    g_ref,
    wg_ref,
):
    tiles = tile_ref.shape[0]
    row_i = lax.broadcasted_iota(jnp.int32, (WIDTH, WIDTH), 0)
    col_i = lax.broadcasted_iota(jnp.int32, (WIDTH, WIDTH), 1)
    tri_ref[...] = jnp.where(row_i < col_i, 1.0, 0.0).astype(BF16)
    tris_ref[...] = jnp.where(row_i > col_i, 1.0, 0.0).astype(BF16)
    acc_ref[...] = jnp.zeros_like(acc_ref)
    words_ref[...] = jnp.zeros_like(words_ref)
    for j, row in enumerate(harmonic_rows(rays_ref[0:1, :], rays_ref[1:2, :], rays_ref[2:3, :])):
        harm_ref[j : j + 1, :] = row
    u = lax.broadcasted_iota(jnp.int32, (SIDE, WIDTH), 0).astype(F32) - (SIDE - 1) * 0.5
    half = WIDTH // 2

    def tile_step(t, carry):
        pix = pl.ds(pl.multiple_of(t * TILE_PIX, TILE_PIX), TILE_PIX)
        src = [tile_ref[t, l] for l in range(LIST)]
        msg = jnp.concatenate([recv_ref[src[l]] for l in range(LIST)], axis=1).astype(F32)
        cu, cv, ca, cb, cc, op = [msg[i : i + 1] for i in range(GEO)]
        high, low = msg[6:7], msg[7:8]
        resid = msg[8:24]
        du = u - cu
        base_u = (-0.5 * LOG2E) * ca * du * du
        cross = (-LOG2E) * cb * du
        curve = (-0.5 * LOG2E) * cc
        for v in range(SIDE):
            rows = slice(v * SIDE, (v + 1) * SIDE)
            dv = (v - (SIDE - 1) * 0.5) - cv
            e = jnp.exp2(base_u + cross * dv + curve * dv * dv)
            lg = jnp.log2(1.0 - op * e)
            lg_hi = lg.astype(BF16)
            e_ref[rows, :] = e
            log_ref[rows, :] = lg_hi
            log_ref[TILE_PIX + v * SIDE : TILE_PIX + (v + 1) * SIDE, :] = (
                lg - lg_hi.astype(F32)
            ).astype(BF16)
        cum_ref[:, :half] = nn(log_ref[:, :half], tri_ref[:half, :half])
        cum_ref[:, half:] = nn(log_ref[...], tri_ref[:, half:])
        for v in range(SIDE):
            rows = slice(v * SIDE, (v + 1) * SIDE)
            cum = cum_ref[rows, :] + cum_ref[TILE_PIX + v * SIDE : TILE_PIX + (v + 1) * SIDE, :]
            wp = jnp.exp2(cum) * e_ref[rows, :]
            wp_ref[rows, :] = wp
            weight = wp * op
            weight_hi = weight.astype(BF16)
            wb_ref[rows, :] = weight_hi
            wl_ref[rows, :] = (weight - weight_hi.astype(F32)).astype(BF16)
        group = jnp.floor(high * 0.25)
        part = high - 4.0 * group
        word_row = lax.broadcasted_iota(jnp.int32, (256, 1), 0).astype(F32)
        for c in range(4):
            key = jnp.where(part == float(c), low, -1.0)
            hot_ref[c * 256 : (c + 1) * 256, :] = jnp.where(word_row == key, 1.0, 0.0).astype(BF16)
        looked_all = nn(book_ref[...], hot_ref[...])
        looked = jnp.where(group == 0.0, looked_all[:COEF], 0.0)
        for g in range(1, GROUPS):
            looked = jnp.where(group == float(g), looked_all[g * COEF : (g + 1) * COEF], looked)
        eight = lax.broadcasted_iota(jnp.int32, (8, WIDTH), 0)
        palette = jnp.concatenate(
            [looked[:16] + resid, looked[16:], jnp.where(eight == 0, 0.5, 0.0)], axis=0
        ).astype(BF16)
        palette = nn(perm_ref[...], palette).astype(BF16)
        mixed = nt(palette, wb_ref[...]) + nt(palette, wl_ref[...])
        harm = harm_ref[:, pix]
        image = jnp.concatenate(
            [
                jnp.sum(harm * mixed[ch * 16 : (ch + 1) * 16], axis=0, keepdims=True)
                + mixed[48:49]
                for ch in range(3)
            ],
            axis=0,
        )
        img_ref[:, pix] = image
        off = image - target_ref[:, pix].astype(F32) / 255.0
        total = off[0:1] + off[1:2] + off[2:3]
        pix8 = lax.broadcasted_iota(jnp.int32, (8, TILE_PIX), 0)
        grad = jnp.concatenate(
            [harm * off[ch : ch + 1] for ch in range(3)] + [jnp.where(pix8 == 0, total, 0.0)],
            axis=0,
        )
        grad_hi = grad.astype(BF16)
        grad_lo = (grad - grad_hi.astype(F32)).astype(BF16)
        g_ref[...] = tn(grad_hi, palette) + tn(grad_lo, palette)
        color = nn(grad_hi, wb_ref[...]) + nn(grad_lo, wb_ref[...]) + nn(grad_hi, wl_ref[...])
        spread = nn(spread_ref[...], color.astype(BF16))
        sixteen = lax.broadcasted_iota(jnp.int32, (16, 1), 0)
        row_group = jnp.where(
            sixteen < 3, 0.0, jnp.where(sixteen < 6, 1.0, jnp.where(sixteen < 9, 2.0, 3.0))
        )
        mask = jnp.where(row_group == group, 1.0, 0.0)
        masked = jnp.concatenate(
            [(spread[i * 16 : (i + 1) * 16] * mask).astype(BF16) for i in range(16)], axis=0
        )
        words_ref[...] += nt(masked, hot_ref[...])
        for v in range(SIDE):
            rows = slice(v * SIDE, (v + 1) * SIDE)
            wg_ref[rows, :] = (wp_ref[rows, :] * g_ref[rows, :] * op).astype(BF16)
        cum_ref[:TILE_PIX, half:] = nn(wg_ref[:, half:], tris_ref[half:, half:])
        cum_ref[:TILE_PIX, :half] = nn(wg_ref[...], tris_ref[:, :half])
        s_zero = jnp.zeros((SIDE, WIDTH), F32)
        s_one = jnp.zeros((SIDE, WIDTH), F32)
        s_two = jnp.zeros((SIDE, WIDTH), F32)
        for v in range(SIDE):
            rows = slice(v * SIDE, (v + 1) * SIDE)
            e = e_ref[rows, :]
            p = wp_ref[rows, :] * g_ref[rows, :] - cum_ref[rows, :] * (e / (1.0 - op * e))
            dv = (v - (SIDE - 1) * 0.5) - cv
            pd = p * dv
            s_zero = s_zero + p
            s_one = s_one + pd
            s_two = s_two + pd * dv
        m_zero = jnp.sum(s_zero, axis=0, keepdims=True)
        m_u = jnp.sum(s_zero * du, axis=0, keepdims=True)
        m_uu = jnp.sum(s_zero * du * du, axis=0, keepdims=True)
        m_v = jnp.sum(s_one, axis=0, keepdims=True)
        m_uv = jnp.sum(s_one * du, axis=0, keepdims=True)
        m_vv = jnp.sum(s_two, axis=0, keepdims=True)
        zero = jnp.zeros((1, WIDTH), F32)
        rows_back = jnp.concatenate(
            [
                color[0:4],
                color[16:20],
                color[32:36],
                op * (ca * m_u + cb * m_v),
                op * (cb * m_u + cc * m_v),
                -0.5 * op * m_uu,
                -op * m_uv,
                -0.5 * op * m_vv,
                m_zero,
                zero,
                zero,
                zero,
                zero,
                zero,
                zero,
            ],
            axis=0,
        )
        for l in range(LIST):
            acc_ref[src[l]] += rows_back[:, l * BLOCK : (l + 1) * BLOCK]
        return carry

    lax.fori_loop(0, tiles, tile_step, 0)

    def finish(j, carry):
        for lane in range(8):
            d = j * 8 + lane
            back_ref[d, 0:16, :] = acc_ref[d, 0:16, :].astype(BF16)
            word = words_ref[
                pl.ds(pl.multiple_of(j * 16, 16), 16), lane * BLOCK : (lane + 1) * BLOCK
            ]
            shifted = pltpu.roll(acc_ref[d, 16:24, :], 4, 0)
            word = jnp.concatenate([word[:8], word[8:] + shifted], axis=0)
            back_ref[d, 16:32, :] = word.astype(BF16)
        return carry

    lax.fori_loop(0, 16, finish, 0)


def render(tile_rows, recv, book, rays, target):
    perm, spread = constants()
    pixels = rays.shape[1]
    n = recv.shape[0]
    return pl.pallas_call(
        render_kernel,
        out_shape=(
            jax.ShapeDtypeStruct((3, pixels), F32),
            jax.ShapeDtypeStruct((n, ROWS_BACK, BLOCK), BF16),
        ),
        in_specs=[pl.BlockSpec(memory_space=pltpu.SMEM)]
        + [pl.BlockSpec(memory_space=pltpu.VMEM)] * 6,
        out_specs=(pl.BlockSpec(memory_space=pltpu.VMEM),) * 2,
        scratch_shapes=[
            pltpu.VMEM((n, 24, BLOCK), F32),
            pltpu.VMEM((256, GWORDS), F32),
            pltpu.VMEM((16, pixels), F32),
            pltpu.VMEM((WIDTH, WIDTH), BF16),
            pltpu.VMEM((WIDTH, WIDTH), BF16),
            pltpu.VMEM((GWORDS, WIDTH), BF16),
            pltpu.VMEM((TILE_PIX, WIDTH), F32),
            pltpu.VMEM((2 * TILE_PIX, WIDTH), BF16),
            pltpu.VMEM((2 * TILE_PIX, WIDTH), F32),
            pltpu.VMEM((TILE_PIX, WIDTH), F32),
            pltpu.VMEM((TILE_PIX, WIDTH), BF16),
            pltpu.VMEM((TILE_PIX, WIDTH), BF16),
            pltpu.VMEM((TILE_PIX, WIDTH), F32),
            pltpu.VMEM((TILE_PIX, WIDTH), BF16),
        ],
        compiler_params=pltpu.CompilerParams(vmem_limit_bytes=48 * 2**20),
        name="render",
    )(tile_rows, recv, book, rays, target, perm, spread)


def owner_kernel(send_ref, back_ref, foot_ref, resid_ref, word_ref, own_ref):
    blocks = own_ref.shape[0]
    own_ref[...] = jnp.zeros_like(own_ref)

    def add(d, words):
        part = back_ref[d].astype(F32)
        b = send_ref[d]
        own_ref[b, 0:16, :] += part[0:16]
        own_ref[b, 16:24, :] += part[24:32]
        return words + part[16:32]

    word_ref[...] = lax.fori_loop(
        0, back_ref.shape[0], add, jnp.zeros((16, BLOCK), F32), unroll=4
    )

    def write(b, carry):
        lanes = pl.ds(pl.multiple_of(b * BLOCK, BLOCK), BLOCK)
        own = own_ref[b]
        resid_ref[:, lanes] = own[0:16].astype(BF16)
        foot_ref[:, lanes] = jnp.concatenate([own[12:16], own[20:22]], axis=0)
        return carry

    lax.fori_loop(0, blocks, write, 0, unroll=4)


def owner_sum(sent, back, blocks):
    return pl.pallas_call(
        owner_kernel,
        out_shape=(
            jax.ShapeDtypeStruct((GEO, blocks * BLOCK), F32),
            jax.ShapeDtypeStruct((16, blocks * BLOCK), BF16),
            jax.ShapeDtypeStruct((16, BLOCK), F32),
        ),
        in_specs=[
            pl.BlockSpec(memory_space=pltpu.SMEM),
            pl.BlockSpec(memory_space=pltpu.VMEM),
        ],
        out_specs=(pl.BlockSpec(memory_space=pltpu.VMEM),) * 3,
        scratch_shapes=[pltpu.VMEM((blocks, 24, BLOCK), F32)],
        name="owner_sum",
    )(sent, back)


def on_device(geometry, codebook, word_ids, residual, send_list, tile_list, rays, target):
    blocks = word_ids.shape[0] // BLOCK
    n_space = lax.axis_size("space")
    sent = send_list[0, 0]
    message = pack(sent, geometry[0], word_ids.reshape(blocks, BLOCK), residual)
    book = lax.all_gather(codebook, "code", axis=0, tiled=True)
    recv = lax.all_to_all(message, "space", split_axis=0, concat_axis=0, tiled=True)
    image, back = render(tile_list[0], recv, book, rays[0], target[0])
    returned = lax.all_to_all(back, "space", split_axis=0, concat_axis=0, tiled=True)
    foot, resid_part, word_part = owner_sum(sent, returned, blocks)
    resid_all = lax.all_gather(resid_part, "code", axis=0)
    resid_sum = jnp.sum(resid_all.astype(F32), axis=0)[:RESID]
    resid_grad = resid_sum.reshape(3, 4, -1).transpose(1, 0, 2).reshape(RESID, -1)
    word_x = lax.all_to_all(
        word_part[:12].reshape(GROUPS, 3 * BLOCK), "code", split_axis=0, concat_axis=0, tiled=True
    )
    word_sum = jnp.sum(word_x, axis=0)
    code = lax.all_gather(word_sum, "space", axis=0).reshape(16, 8, 3, BLOCK)
    code_grad = code.transpose(0, 2, 1, 3).reshape(COEF, GWORDS)
    return (image[None], foot[None], resid_grad, code_grad)


def solution(mesh):
    placed = (
        P("code", None, "space"),
        P(None, "code"),
        P("space"),
        P(None, "space"),
        P("code", "space", None),
        P("code", "space", None),
        P("code", None, "space"),
        P("code", None, "space"),
    )
    return jax.shard_map(
        on_device,
        mesh=mesh,
        in_specs=placed,
        out_specs=(
            P("code", None, "space"),
            P("code", None, "space"),
            P(None, "space"),
            P(None, "code"),
        ),
        check_vma=False,
    )
```

time: 952 us -> 273 us (0.29)
  waiting for transfers between devices: 491 us -> 31.5 us
  other arithmetic: 108 us -> 1.44 us
  local copies, waits for them, and re-layouts: 69 us -> 6.01 us
  matrix products: 40.4 us -> 0 us
  Pallas kernels: 0 us -> 24.1 us
  blocking collectives: 187 us -> 171 us
  starting transfers between devices: 38.4 us -> 24.8 us
    psum x2 -> x0, waiting for transfers between devices: 386 us -> none  [the longest x1 331 us: on_device(): code_grad = lax.psum(codeword_portion, 'space')]
    all_to_all x1, blocking collectives: 173 us -> 61.2 us  [on_device(): lax.all_to_all(back, 'space', split_axis=0, concat_axis=0, tiled=True)]
    all_gather x1 -> x2, blocking collectives: 13.4 us -> 110 us  [the longest x1 98.2 us: on_device(): code = lax.all_gather(word_sum, 'space', axis=0).reshape(16, 8, 3, BLOCK)]
    scatter-add x1 -> x0, other arithmetic: 45.7 us -> none  [on_device(): jax.ops.segment_sum(palette_owned.T, word_ids, num_segments=WORDS)]
    dot_general x14 -> x0, matrix products: 40.4 us -> none  [the longest x12 33.9 us: composite(): mixed = jnp.dot(weight, palette.T, precision=lax.Precision.HIGHEST)]
    all_to_all x2, waiting for transfers between devices: 70.4 us -> 31.5 us  [the longest x1 29.8 us: on_device(): lax.all_to_all(message, 'space', split_axis=0, concat_axis=0, tiled=True)]
    reduce_scatter x1 -> x0, waiting for transfers between devices: 34.8 us -> none  [on_device(): lax.psum_scatter(word_term, 'code', scatter_dimension=1, tiled=True)]
    gather x10 -> x0, local copies, waits for them, and re-layouts: 32.9 us -> none  [the longest x2 28.8 us: decode(): looked = jnp.take(codebook, word_ids, axis=1).astype(jnp.float32)]
  transfers between devices with their start and end apart: 5 -> 3, of which waited for: 4 -> 2; matrix products, arithmetic and copies ran while one was open for 4% -> 1% of each run, Pallas kernels for 0% -> 0%
where the time goes in v1:
time: 273 us
  blocking collectives  171 us (63%)
  waiting for transfers between devices  31.5 us (12%)
  starting transfers between devices  24.8 us (9%)
  Pallas kernels  24.1 us (9%)
  between operations  14.1 us (5%)
  local copies, waits for them, and re-layouts  6.01 us (2%)
    all_gather x1, blocking collectives, on_device(): code = lax.all_gather(word_sum, 'space', axis=0).reshape(16, 8, 3, BLOCK)  98.2 us
    all_to_all x1, blocking collectives, on_device(): lax.all_to_all(back, 'space', split_axis=0, concat_axis=0, tiled=True)  61.2 us
    all_to_all x1, waiting for transfers between devices, on_device(): lax.all_to_all(message, 'space', split_axis=0, concat_axis=0, tiled=True)  29.8 us
    all_to_all x1, starting transfers between devices, on_device(): lax.all_to_all(message, 'space', split_axis=0, concat_axis=0, tiled=True)  20.7 us
    pallas_call x1, Pallas kernels, render(): pl.pallas_call(render_kernel, out_shape=(jax.ShapeDtypeStruct((3, pixels)...  18.9 us
    all_gather x1, blocking collectives, on_device(): book = lax.all_gather(codebook, 'code', axis=0, tiled=True)  11.4 us
  transfers between devices with their start and end apart: 3, of which 2 were waited for; matrix products, arithmetic and copies ran while one was open for 1% of the time, Pallas kernels for 0%

profile of v1, /device:TPU:1, one launch (start us, length us, event | category | flops | bytes accessed | tf_op | source)
XLA Modules:
  0.0 272.8 jit_solution(14668246295678944609)
XLA Ops:
  7.2 2.4 pack.1
  9.5 0.0 copy-start
  9.5 0.0 copy-start.1
  9.6 20.7 %all-to-all-start = ((bf16[128,24,128]{2,1,0:T(8,128)(2,1)}), bf16[128,24,128]{2,1,0:T(8,128)(2,1)S(1)}, u32[]{:S(2)}, u32[]{:S(2)}) async-start(bf16[128,24,128]{2,1,0:T(8,128)(2,1)} %pack.1), calls=%async_computation | async-start | bytes 1572864 | tf_op jit(solution)/shard_map/all_to_all | solution.py:402
  30.3 0.0 all-gather.5.cloned.1.call-start
  30.3 0.1 copy.21.tile_ref
  30.5 11.4 %all_gather.15.book_ref = bf16[192,1024]{1,0:T(8,128)(2,1)S(1)} all-gather(bf16[48,1024]{1,0:T(8,128)(2,1)S(1)} %copy-done.2), channel_id=1, replica_groups=mesh['space'=128,'code'=4] {'code'}, dimensions={0}, use_global_device_ids=true | all-gather | bytes 491520 | tf_op jit(solution)/shard_map/all_gather | solution.py:401
  41.9 29.8 %all-to-all-done.recv_ref = bf16[128,24,128]{2,1,0:T(8,128)(2,1)S(1)} async-done(((bf16[128,24,128]{2,1,0:T(8,128)(2,1)}), bf16[128,24,128]{2,1,0:T(8,128)(2,1)S(1)}, u32[]{:S(2)}, u32[]{:S(2)}) %all-to-all-start) | async-done | bytes 786464 | tf_op jit(solution)/shard_map/all_to_all | solution.py:402
  71.7 0.0 copy-done.1
  71.7 18.9 %render.1 = (f32[3,2048]{1,0:T(4,128)S(1)}, bf16[128,32,128]{2,1,0:T(8,128)(2,1)S(1)}) custom-call(s32[8,4]{1,0:T(8,128)S(1)} %copy.21.tile_ref, bf16[128,24,128]{2,1,0:T(8,128)(2,1)S(1)} %all-to-all-done.recv_ref, bf16[192,1024]{1,0:T(8,128)(2,1)S(1)} %all_gather.15.book_ref, f32[3,2048]{1,0:T(4,128)S(1)} %bitcast.25, s32[3,2048]{1,0:T(4,128)S(1)} %bitcast.26, ...), custom_call_target="tpu_custom_call" | custom-call | tf_op jit(solution)/shard_map/render/pallas_call | solution.py:323
  90.7 61.2 %all_to_all.20.back_ref = bf16[128,32,128]{2,1,0:T(8,128)(2,1)} all-to-all(bf16[128,32,128]{2,1,0:T(8,128)(2,1)S(1)} %get-tuple-element.10), channel_id=1, replica_groups=mesh['space'=128,'code'=4] {'space'}, dimensions={0} | all-to-all | bytes 2097152 | tf_op jit(solution)/shard_map/all_to_all | solution.py:404
  151.9 2.8 %owner_sum.1 = (f32[6,8192]{1,0:T(8,128)}, bf16[16,8192]{1,0:T(8,128)(2,1)}, f32[16,128]{1,0:T(8,128)}) custom-call(s32[128]{0:T(128)} %bitcast.38, bf16[128,32,128]{2,1,0:T(8,128)(2,1)} %all_to_all.20.back_ref), custom_call_target="tpu_custom_call" | custom-call | tf_op jit(solution)/shard_map/owner_sum/pallas_call | solution.py:379
  154.7 0.0 all-gather.5.cloned.1.call-update
  154.7 1.3 all_to_all.16
  156.0 4.0 %all-to-all-start.2 = ((f32[4,1,384]{2,1,0:T(1,128)}), f32[4,1,384]{2,1,0:T(1,128)S(1)}, u32[]{:S(2)}, u32[]{:S(2)}) async-start(f32[4,1,384]{2,1,0:T(1,128)} %all_to_all.16), calls=%async_computation.2 | async-start | bytes 12288 | tf_op jit(solution)/shard_map/all_to_all | solution.py:409
  160.1 0.6 copy.25
  160.7 1.8 copy.26
  162.5 1.7 all-to-all-done.2
  164.2 98.2 %all-gather.2 = f32[128,1,384]{2,1,0:T(1,128)S(1)} all-gather(f32[1,1,384]{2,1,0:T(1,128)S(1)} %reshape.36), channel_id=3, replica_groups=mesh['space'=128,'code'=4] {'space'}, dimensions={0}, use_global_device_ids=true | all-gather | bytes 198144 | tf_op jit(solution)/shard_map/all_gather | solution.py:413
  262.4 0.7 copy.33
  263.1 1.4 convert_reduce_fusion
  264.6 0.1 reshape.28
  264.7 0.3 copy.22
  265.0 1.0 reshape.29
  (15 shorter events, 0.1 us)
Async XLA Ops:
  9.5 20.8 %copy-start.5 = (s32[1,8,4]{1,2,0:T(4,128)S(1)}, s32[1,8,4]{1,2,0:T(4,128)}, u32[]{:S(2)}) copy-start(s32[1,8,4]{1,2,0:T(4,128)} %param.15) | copy-start | bytes 388
  9.5 20.9 %copy-start.3 = (f32[1,3,2048]{2,0,1:T(1,128)S(1)}, f32[1,3,2048]{2,0,1:T(1,128)}, u32[]{:S(2)}) copy-start(f32[1,3,2048]{2,0,1:T(1,128)} %param.16) | copy-start | bytes 73732
  9.5 20.9 %copy-start.4 = (s32[1,3,2048]{2,0,1:T(1,128)S(1)}, s32[1,3,2048]{2,0,1:T(1,128)}, u32[]{:S(2)}) copy-start(s32[1,3,2048]{2,0,1:T(1,128)} %param.17) | copy-start | bytes 73732
  9.5 20.9 %copy-start.2 = (bf16[48,1024]{1,0:T(8,128)(2,1)S(1)}, bf16[48,1024]{1,0:T(8,128)(2,1)}, u32[]{:S(2)}) copy-start(bf16[48,1024]{1,0:T(8,128)(2,1)} %param.11) | copy-start | bytes 294916
  9.5 62.2 %copy-start = (bf16[256,56]{1,0:T(8,128)(2,1)S(1)}, bf16[256,56]{1,0:T(8,128)(2,1)}, u32[]{:S(2)}) copy-start(bf16[256,56]{1,0:T(8,128)(2,1)} %constant.7.clone.spread_ref) | copy-start | bytes 86020
  9.5 62.1 %copy-start.1 = (bf16[56,56]{1,0:T(8,128)(2,1)S(1)}, bf16[56,56]{1,0:T(8,128)(2,1)}, u32[]{:S(2)}) copy-start(bf16[56,56]{1,0:T(8,128)(2,1)} %constant.6.clone.perm_ref) | copy-start | bytes 18820
  9.6 62.1 %all-to-all-start = ((bf16[128,24,128]{2,1,0:T(8,128)(2,1)}), bf16[128,24,128]{2,1,0:T(8,128)(2,1)S(1)}, u32[]{:S(2)}, u32[]{:S(2)}) async-start(bf16[128,24,128]{2,1,0:T(8,128)(2,1)} %pack.1), calls=%async_computation | async-start | bytes 1572864 | tf_op jit(solution)/shard_map/all_to_all | solution.py:402
  30.3 232.9 %all-gather.5.cloned.1.call-start = ((), (), s32[]{:S(2)}) async-start(), calls=%async_computation.3 | async-start | bytes 1310720 | tf_op jit(solution)/shard_map/all_gather | solution.py:406
  156.0 8.2 %all-to-all-start.2 = ((f32[4,1,384]{2,1,0:T(1,128)}), f32[4,1,384]{2,1,0:T(1,128)S(1)}, u32[]{:S(2)}, u32[]{:S(2)}) async-start(f32[4,1,384]{2,1,0:T(1,128)} %all_to_all.16), calls=%async_computation.2 | async-start | bytes 12288 | tf_op jit(solution)/shard_map/all_to_all | solution.py:409
Sparse Core Ops, SparseCore 0:
  154.8 25.6 all-gather.4

commit v2 on v1

v2 whole, which is shorter than its diff:
```python
import functools

import jax
import jax.numpy as jnp
import numpy as np
from jax import lax
from jax.experimental import pallas as pl
from jax.experimental.pallas import tpu as pltpu
from jax.sharding import PartitionSpec as P

WORDS = 4096
COEF = 48
RESID = 12
GEO = 6
BLOCK = 128
LIST = 4
SIDE = 16
TILE_PIX = 256
WIDTH = LIST * BLOCK
GROUPS = 4
GWORDS = WORDS // GROUPS
PAIRS_B = RESID // 2
PAIRS_T = 5
STAGE = 16
LOG2E = 1.4426950408889634
F32 = jnp.float32
BF16 = jnp.bfloat16
MESH = pl.DeviceIdType.MESH

band_zero = 0.28209479177387814
band_one = 0.4886025119029199
band_two = (
    1.0925484305920792,
    -1.0925484305920792,
    0.31539156525252005,
    -1.0925484305920792,
    0.5462742152960396,
)
band_three = (
    -0.5900435899266435,
    2.890611442640554,
    -0.4570457994644658,
    0.3731763325901154,
    -0.4570457994644658,
    1.445305721320277,
    -0.5900435899266435,
)


def harmonic_rows(ray_x, ray_y, ray_z):
    length = jnp.sqrt(ray_x * ray_x + ray_y * ray_y + ray_z * ray_z)
    x = ray_x / length
    y = ray_y / length
    z = ray_z / length
    xx, yy, zz = x * x, y * y, z * z
    return [
        band_zero * jnp.ones_like(x),
        -band_one * y,
        band_one * z,
        -band_one * x,
        band_two[0] * x * y,
        band_two[1] * y * z,
        band_two[2] * (2.0 * zz - xx - yy),
        band_two[3] * x * z,
        band_two[4] * (xx - yy),
        band_three[0] * y * (3.0 * xx - yy),
        band_three[1] * x * y * z,
        band_three[2] * y * (4.0 * zz - xx - yy),
        band_three[3] * z * (2.0 * zz - 3.0 * xx - 3.0 * yy),
        band_three[4] * x * (4.0 * zz - xx - yy),
        band_three[5] * z * (xx - yy),
        band_three[6] * x * (xx - 3.0 * yy),
    ]


def nn(a, b):
    return lax.dot_general(a, b, (((1,), (0,)), ((), ())), preferred_element_type=F32)


def nt(a, b):
    return lax.dot_general(a, b, (((1,), (1,)), ((), ())), preferred_element_type=F32)


def tn(a, b):
    return lax.dot_general(a, b, (((0,), (0,)), ((), ())), preferred_element_type=F32)


def greet(n_space, n_code):
    me, x = lax.axis_index("space"), lax.axis_index("code")
    barrier = pltpu.get_barrier_semaphore()

    def hello(k, carry):
        pl.semaphore_signal(
            barrier, inc=1, device_id={"space": lax.rem(me + k, n_space)}, device_id_type=MESH
        )
        return carry

    lax.fori_loop(1, n_space, hello, 0)
    for k in range(1, n_code):
        pl.semaphore_signal(
            barrier, inc=1, device_id={"code": lax.rem(x + k, n_code)}, device_id_type=MESH
        )
    return barrier


def to_space(n_space, fill, src, dst, send_sem, recv_sem):
    me = lax.axis_index("space")

    def one(d):
        if fill is not None:
            fill(d)
        pltpu.make_async_remote_copy(
            src_ref=src.at[d],
            dst_ref=dst.at[me],
            send_sem=send_sem,
            recv_sem=recv_sem,
            device_id={"space": d},
            device_id_type=MESH,
        ).start()

    def pair(k, carry):
        one(lax.rem(me + k, n_space))
        one(lax.rem(me + n_space - k, n_space))
        return carry

    lax.fori_loop(1, n_space // 2, pair, 0)
    one(lax.rem(me + n_space // 2, n_space))


def all_of(n_space, src, dst, send_sem, recv_sem):
    me = lax.axis_index("space")
    return pltpu.make_async_remote_copy(
        src_ref=src.at[pl.ds(0, n_space - 1)],
        dst_ref=dst.at[pl.ds(0, n_space - 1)],
        send_sem=send_sem,
        recv_sem=recv_sem,
        device_id={"space": lax.rem(me + 1, n_space)},
        device_id_type=MESH,
    )


def constants():
    perm = np.zeros((56, 56), np.float32)
    for j in range(16):
        for ch in range(3):
            perm[ch * 16 + j, 3 * j + ch] = 1.0
    perm[48, 48] = 1.0
    spread = np.zeros((128, COEF), np.float32)
    for k in range(COEF):
        spread[k // 3 * 8 + k % 3, k] = 1.0
    return jnp.asarray(perm, BF16), jnp.asarray(spread, BF16)


def put_rows(ref, row, value):
    ref[pl.ds(row, value.shape[0], stride=STAGE), :] = value


def get_rows(ref, row, count):
    return ref[pl.ds(row, count, stride=STAGE), :]


def step_kernel(
    n_space,
    n_code,
    send_ref,
    tile_ref,
    send_row_ref,
    tile_row_ref,
    geo_ref,
    word_ref,
    resid_ref,
    code_ref,
    rays_ref,
    target_ref,
    perm_ref,
    spread_ref,
    img_ref,
    foot_ref,
    resid_out_ref,
    code_out_ref,
    blocks_a,
    blocks_b,
    msg_a,
    msg_b,
    recv_a,
    recv_b,
    book_ref,
    e_ref,
    wp_ref,
    wb_ref,
    wl_ref,
    g_ref,
    hot_ref,
    look_ref,
    natural_ref,
    log_ref,
    cum_ref,
    wg_ref,
    tri_ref,
    tris_ref,
    harm_ref,
    words_ref,
    mine_ref,
    theirs_ref,
    wide_ref,
    grads_ref,
    stage_ref,
    stage_t_ref,
    msg_r,
    recv_r,
    msg_t,
    recv_t,
    own_ref,
    own_resid_ref,
    part_ref,
    line_ref,
    lines_ref,
    sems,
    code_send,
    code_recv,
    near_send,
    near_recv,
    far_send,
    far_recv,
):
    me, x = lax.axis_index("space"), lax.axis_index("code")
    tiles = tile_ref.shape[0]
    slots = tiles * LIST
    blocks = blocks_a.shape[0]
    half = WIDTH // 2
    barrier = greet(n_space, n_code)

    def lanes_of(i, width=BLOCK):
        return pl.ds(pl.multiple_of(i * width, width), width)

    def build(b, carry):
        ids = word_ref[pl.ds(b, 1), :]
        high = (ids >> 8).astype(F32)
        low = (ids & 255).astype(F32)
        geo = geo_ref[:, lanes_of(b)].astype(F32)
        blocks_a[b] = jnp.concatenate([geo, high, low], axis=0).astype(BF16)
        resid = resid_ref[:, lanes_of(b)].astype(F32)
        blocks_b[b] = jnp.concatenate(
            [resid[2 * i : 2 * i + 2] for i in range(PAIRS_B)], axis=1
        ).astype(BF16)
        return carry

    lax.fori_loop(0, blocks, build, 0, unroll=4)
    book_ref[x] = code_ref[...]
    pl.semaphore_wait(barrier, n_space + n_code - 2)

    def around(src, dst, first):
        copies = []
        for k in range(1, n_code):
            copies.append(
                pltpu.make_async_remote_copy(
                    src_ref=src(k),
                    dst_ref=dst(k),
                    send_sem=code_send.at[first + k - 1],
                    recv_sem=code_recv.at[first + k - 1],
                    device_id={"code": lax.rem(x + k, n_code)},
                    device_id_type=MESH,
                )
            )
            copies[-1].start()
        return copies

    def finish(src, dst, first):
        every = all_of(n_space, src, dst, sems.at[first], sems.at[first + 1])
        every.wait_recv()
        return every

    book_copies = around(lambda k: code_ref, lambda k: book_ref.at[x], 0)

    def fill_a(d):
        msg_a[d] = blocks_a[send_ref[d]]

    def fill_b(d):
        msg_b[d] = blocks_b[send_ref[d]]

    to_space(n_space, fill_a, msg_a, recv_a, sems.at[0], sems.at[1])
    to_space(n_space, fill_b, msg_b, recv_b, sems.at[2], sems.at[3])
    recv_a[me] = blocks_a[send_ref[me]]
    recv_b[me] = blocks_b[send_ref[me]]

    row_i = lax.broadcasted_iota(jnp.int32, (WIDTH, WIDTH), 0)
    col_i = lax.broadcasted_iota(jnp.int32, (WIDTH, WIDTH), 1)
    tri_ref[...] = jnp.where(row_i < col_i, 1.0, 0.0).astype(BF16)
    tris_ref[...] = jnp.where(row_i > col_i, 1.0, 0.0).astype(BF16)
    for j, row in enumerate(harmonic_rows(rays_ref[0:1, :], rays_ref[1:2, :], rays_ref[2:3, :])):
        harm_ref[j : j + 1, :] = row
    words_ref[...] = jnp.zeros_like(words_ref)
    u = lax.broadcasted_iota(jnp.int32, (SIDE, WIDTH), 0).astype(F32) - (SIDE - 1) * 0.5

    def message(t):
        return jnp.concatenate([recv_a[tile_ref[t, l]] for l in range(LIST)], axis=1).astype(F32)

    def v_rows(t, v):
        return pl.ds(pl.multiple_of(t * TILE_PIX + v * SIDE, SIDE), SIDE)

    def absorb_step(t, carry):
        msg = message(t)
        cu, cv, ca, cb, cc, op = [msg[i : i + 1] for i in range(GEO)]
        high, low = msg[6:7], msg[7:8]
        du = u - cu
        base_u = (-0.5 * LOG2E) * ca * du * du
        cross = (-LOG2E) * cb * du
        curve = (-0.5 * LOG2E) * cc
        for v in range(SIDE):
            rows = slice(v * SIDE, (v + 1) * SIDE)
            dv = (v - (SIDE - 1) * 0.5) - cv
            e = jnp.exp2(base_u + cross * dv + curve * dv * dv)
            lg = jnp.log2(1.0 - op * e)
            lg_hi = lg.astype(BF16)
            e_ref[v_rows(t, v), :] = e
            log_ref[rows, :] = lg_hi
            log_ref[TILE_PIX + v * SIDE : TILE_PIX + (v + 1) * SIDE, :] = (
                lg - lg_hi.astype(F32)
            ).astype(BF16)
        cum_ref[:, :half] = nn(log_ref[:, :half], tri_ref[:half, :half])
        cum_ref[:, half:] = nn(log_ref[...], tri_ref[:, half:])
        for v in range(SIDE):
            rows = slice(v * SIDE, (v + 1) * SIDE)
            cum = cum_ref[rows, :] + cum_ref[TILE_PIX + v * SIDE : TILE_PIX + (v + 1) * SIDE, :]
            wp = jnp.exp2(cum) * e_ref[v_rows(t, v), :]
            wp_ref[v_rows(t, v), :] = wp
            weight = wp * op
            weight_hi = weight.astype(BF16)
            wb_ref[v_rows(t, v), :] = weight_hi
            wl_ref[v_rows(t, v), :] = (weight - weight_hi.astype(F32)).astype(BF16)
        group = jnp.floor(high * 0.25)
        part = high - 4.0 * group
        word_row = lax.broadcasted_iota(jnp.int32, (256, 1), 0).astype(F32)
        for c in range(4):
            key = jnp.where(part == float(c), low, -1.0)
            hot_ref[t, c * 256 : (c + 1) * 256, :] = jnp.where(word_row == key, 1.0, 0.0).astype(
                BF16
            )
        looked_all = nn(book_ref[...].reshape(n_code * COEF, GWORDS), hot_ref[t])
        looked = jnp.where(group == 0.0, looked_all[:COEF], 0.0)
        for g in range(1, GROUPS):
            looked = jnp.where(group == float(g), looked_all[g * COEF : (g + 1) * COEF], looked)
        look_ref[t] = looked.astype(BF16)
        return carry

    for copy in book_copies:
        copy.wait()
    every_a = finish(msg_a, recv_a, 0)
    lax.fori_loop(0, tiles, absorb_step, 0)

    def unpair(ref, d):
        pairs = ref[d].astype(F32)
        rows = [pairs[:, i * BLOCK : (i + 1) * BLOCK] for i in range(PAIRS_B)]
        return jnp.concatenate(rows + [jnp.zeros((16 - RESID, BLOCK), F32)], axis=0)

    def color_step(t, carry):
        pix = lanes_of(t, TILE_PIX)
        resid = jnp.concatenate([unpair(recv_b, tile_ref[t, l]) for l in range(LIST)], axis=1)
        looked = look_ref[t].astype(F32)
        eight = lax.broadcasted_iota(jnp.int32, (8, WIDTH), 0)
        palette = jnp.concatenate(
            [looked[:16] + resid, looked[16:], jnp.where(eight == 0, 0.5, 0.0)], axis=0
        ).astype(BF16)
        palette = nn(perm_ref[...], palette).astype(BF16)
        weight = wb_ref[pix, :]
        weight_lo = wl_ref[pix, :]
        mixed = nt(palette, weight) + nt(palette, weight_lo)
        harm = harm_ref[:, pix]
        image = jnp.concatenate(
            [
                jnp.sum(harm * mixed[ch * 16 : (ch + 1) * 16], axis=0, keepdims=True)
                + mixed[48:49]
                for ch in range(3)
            ],
            axis=0,
        )
        img_ref[:, pix] = image
        off = image - target_ref[:, pix].astype(F32) / 255.0
        total = off[0:1] + off[1:2] + off[2:3]
        pix8 = lax.broadcasted_iota(jnp.int32, (8, TILE_PIX), 0)
        grad = jnp.concatenate(
            [harm * off[ch : ch + 1] for ch in range(3)] + [jnp.where(pix8 == 0, total, 0.0)],
            axis=0,
        )
        grad_hi = grad.astype(BF16)
        grad_lo = (grad - grad_hi.astype(F32)).astype(BF16)
        g_ref[pix, :] = tn(grad_hi, palette) + tn(grad_lo, palette)
        color = nn(grad_hi, weight) + nn(grad_lo, weight) + nn(grad_hi, weight_lo)
        natural_ref[t] = tn(perm_ref[...], color.astype(BF16))[:COEF].astype(BF16)
        for j in range(4):
            for ch in range(3):
                row = color[ch * 16 + j : ch * 16 + j + 1]
                for l in range(LIST):
                    grads_ref[pl.ds((3 * j + ch) * slots + t * LIST + l, 1), :] = row[
                        :, l * BLOCK : (l + 1) * BLOCK
                    ]
        return carry

    every_b = finish(msg_b, recv_b, 2)
    lax.fori_loop(0, tiles, color_step, 0)

    slot_d = lax.broadcasted_iota(jnp.int32, (n_space, slots), 0)
    slot_hot = jnp.where(slot_d == tile_row_ref[...], 1.0, 0.0)
    slot_hot = jnp.concatenate([slot_hot, slot_hot], axis=1).astype(BF16)

    def to_slots(r, ref, row):
        part = grads_ref[r * slots : (r + 1) * slots, :]
        part_hi = part.astype(BF16).astype(F32)
        both = jnp.concatenate([part_hi, part - part_hi], axis=0).astype(BF16)
        put_rows(ref, row, nn(slot_hot, both))

    for r in range(RESID):
        to_slots(r, stage_ref, r)

    def fill_r(d):
        for i in range(PAIRS_B):
            msg_r[d, :, i * BLOCK : (i + 1) * BLOCK] = stage_ref[
                pl.ds(pl.multiple_of(d * STAGE, STAGE) + 2 * i, 2), :
            ].astype(BF16)

    to_space(n_space, fill_r, msg_r, recv_r, sems.at[4], sems.at[5])
    fill_r(me)
    recv_r[me] = msg_r[me]

    def word_step(t, carry):
        group = jnp.floor(message(t)[6:7] * 0.25)
        natural = natural_ref[t].astype(F32)
        masked = jnp.concatenate(
            [jnp.where(group == float(g), natural, 0.0).astype(BF16) for g in range(GROUPS)], axis=0
        )
        words_ref[...] += nt(masked, hot_ref[t])
        return carry

    lax.fori_loop(0, tiles, word_step, 0)
    for g in range(GROUPS):
        mine_ref[g] = words_ref[g * COEF : (g + 1) * COEF, :].astype(BF16)
    word_copies = around(
        lambda k: mine_ref.at[lax.rem(x + k, n_code)], lambda k: theirs_ref.at[k - 1], 3
    )

    def foot_step(t, carry):
        msg = message(t)
        cu, cv, ca, cb, cc, op = [msg[i : i + 1] for i in range(GEO)]
        du = u - cu
        for v in range(SIDE):
            rows = slice(v * SIDE, (v + 1) * SIDE)
            wg_ref[rows, :] = (wp_ref[v_rows(t, v), :] * g_ref[v_rows(t, v), :] * op).astype(BF16)
        cum_ref[:TILE_PIX, half:] = nn(wg_ref[:, half:], tris_ref[half:, half:])
        cum_ref[:TILE_PIX, :half] = nn(wg_ref[...], tris_ref[:, :half])
        s_zero = jnp.zeros((SIDE, WIDTH), F32)
        s_one = jnp.zeros((SIDE, WIDTH), F32)
        s_two = jnp.zeros((SIDE, WIDTH), F32)
        for v in range(SIDE):
            rows = slice(v * SIDE, (v + 1) * SIDE)
            e = e_ref[v_rows(t, v), :]
            p = wp_ref[v_rows(t, v), :] * g_ref[v_rows(t, v), :] - cum_ref[rows, :] * (
                e / (1.0 - op * e)
            )
            dv = (v - (SIDE - 1) * 0.5) - cv
            pd = p * dv
            s_zero = s_zero + p
            s_one = s_one + pd
            s_two = s_two + pd * dv
        m_zero = jnp.sum(s_zero, axis=0, keepdims=True)
        m_u = jnp.sum(s_zero * du, axis=0, keepdims=True)
        m_uu = jnp.sum(s_zero * du * du, axis=0, keepdims=True)
        m_v = jnp.sum(s_one, axis=0, keepdims=True)
        m_uv = jnp.sum(s_one * du, axis=0, keepdims=True)
        m_vv = jnp.sum(s_two, axis=0, keepdims=True)
        rows_back = [
            op * (ca * m_u + cb * m_v),
            op * (cb * m_u + cc * m_v),
            -0.5 * op * m_uu,
            -op * m_uv,
            -0.5 * op * m_vv,
            m_zero,
        ]
        for r, row in enumerate(rows_back):
            for l in range(LIST):
                grads_ref[pl.ds((RESID + r) * slots + t * LIST + l, 1), :] = row[
                    :, l * BLOCK : (l + 1) * BLOCK
                ]
        return carry

    lax.fori_loop(0, tiles, foot_step, 0)
    for r in range(GEO):
        to_slots(RESID + r, stage_t_ref, 4 + r)
    for copy in word_copies:
        copy.wait()
    total = words_ref[pl.ds(pl.multiple_of(x * COEF, COEF), COEF), :]
    for k in range(n_code - 1):
        total = total + theirs_ref[k].astype(F32)
    wide_ref[...] = nn(spread_ref[...], total.astype(BF16))
    row8 = lax.broadcasted_iota(jnp.int32, (8, BLOCK), 0)

    def fill_t(d):
        own = pl.ds(pl.multiple_of(d * STAGE, STAGE), 8)
        word = wide_ref[pl.ds(pl.multiple_of(d // 8 * 8, 8), 8), lanes_of(lax.rem(d, 8))]
        stage_t_ref[own, :] = jnp.where(row8 < 4, word, stage_t_ref[own, :])
        for i in range(PAIRS_T):
            msg_t[d, :, i * BLOCK : (i + 1) * BLOCK] = stage_t_ref[
                pl.ds(pl.multiple_of(d * STAGE, STAGE) + 2 * i, 2), :
            ].astype(BF16)

    to_space(n_space, fill_t, msg_t, recv_t, sems.at[6], sems.at[7])
    fill_t(me)
    recv_t[me] = msg_t[me]

    own_b = lax.broadcasted_iota(jnp.int32, (blocks + 8, n_space), 0)
    own_hot = jnp.where(own_b == send_row_ref[...], 1.0, 0.0)
    own_hot = jnp.where(own_b == blocks, 1.0, own_hot).astype(BF16)

    def spread_pairs(ref, stage, pairs):
        def one(d, carry):
            for i in range(pairs):
                stage[pl.ds(pl.multiple_of(d * STAGE, STAGE) + 2 * i, 2), :] = ref[
                    d, :, i * BLOCK : (i + 1) * BLOCK
                ].astype(F32)
            return carry

        lax.fori_loop(0, n_space, one, 0, unroll=4)

    def owned(stage, row):
        return nn(own_hot, get_rows(stage, row, n_space).astype(BF16))

    every_r = finish(msg_r, recv_r, 4)
    spread_pairs(recv_r, stage_ref, PAIRS_B)
    for r in range(RESID):
        put_rows(own_ref, r, owned(stage_ref, r)[:blocks])

    def write_resid(b, carry):
        own_resid_ref[:, lanes_of(b)] = own_ref[pl.ds(pl.multiple_of(b * STAGE, STAGE), STAGE), :][
            :RESID
        ]
        return carry

    lax.fori_loop(0, blocks, write_resid, 0, unroll=4)
    width = part_ref.shape[2]
    resid_copies = around(
        lambda k: own_resid_ref.at[:, lanes_of(lax.rem(x + k, n_code), width)],
        lambda k: part_ref.at[k - 1],
        6,
    )
    for copy in resid_copies:
        copy.wait()
    total = own_resid_ref[:, lanes_of(x, width)]
    for k in range(n_code - 1):
        total = total + part_ref[k]
    resid_out_ref[:, lanes_of(x, width)] = total
    resid_copies = around(
        lambda k: resid_out_ref.at[:, lanes_of(x, width)],
        lambda k: resid_out_ref.at[:, lanes_of(x, width)],
        9,
    )

    every_t = finish(msg_t, recv_t, 6)
    spread_pairs(recv_t, stage_t_ref, PAIRS_T)
    line_ref[...] = jnp.concatenate(
        [owned(stage_t_ref, r)[blocks : blocks + 1] for r in range(3)], axis=1
    )
    plane, place = me // 8, lax.rem(me, 8)
    lines_ref[plane, place] = line_ref[...]
    near = []
    for k in range(1, 8):
        near.append(
            pltpu.make_async_remote_copy(
                src_ref=line_ref,
                dst_ref=lines_ref.at[plane, place],
                send_sem=near_send.at[k - 1],
                recv_sem=near_recv.at[k - 1],
                device_id={"space": plane * 8 + lax.rem(place + k, 8)},
                device_id_type=MESH,
            )
        )
        near[-1].start()
    for copy in near:
        copy.wait()
    planes = n_space // 8
    far = []
    for k in range(1, planes):
        far.append(
            pltpu.make_async_remote_copy(
                src_ref=lines_ref.at[plane],
                dst_ref=lines_ref.at[plane],
                send_sem=far_send.at[k - 1],
                recv_sem=far_recv.at[k - 1],
                device_id={"space": lax.rem(plane + k, planes) * 8 + place},
                device_id_type=MESH,
            )
        )
        far[-1].start()
    for r in range(GEO):
        put_rows(own_ref, r, owned(stage_t_ref, 4 + r)[:blocks])

    def write_foot(b, carry):
        foot_ref[:, lanes_of(b)] = own_ref[pl.ds(pl.multiple_of(b * STAGE, STAGE), 8), :][:GEO]
        return carry

    lax.fori_loop(0, blocks, write_foot, 0, unroll=4)
    for copy in far:
        copy.wait()
    for d in range(n_space):
        for i in range(3):
            row = d // 8 * 3 + i
            code_out_ref[row : row + 1, d % 8 * BLOCK : (d % 8 + 1) * BLOCK] = lines_ref[
                d // 8, d % 8, :, i * BLOCK : (i + 1) * BLOCK
            ]
    for copy in resid_copies:
        copy.wait()
    for every in (every_a, every_b, every_r, every_t):
        every.wait_send()


def on_device(geometry, codebook, word_ids, residual, send_list, tile_list, rays, target):
    blocks = word_ids.shape[0] // BLOCK
    n_space = lax.axis_size("space")
    n_code = lax.axis_size("code")
    perm, spread = constants()
    tiles = tile_list.shape[1]
    pixels = rays.shape[2]
    splats = blocks * BLOCK
    sent = send_list[0, 0]
    vm = pltpu.VMEM
    dma = pltpu.SemaphoreType.DMA
    image, foot, resid_grad, code_grad = pl.pallas_call(
        functools.partial(step_kernel, n_space, n_code),
        out_shape=(
            jax.ShapeDtypeStruct((3, pixels), F32),
            jax.ShapeDtypeStruct((GEO, splats), F32),
            jax.ShapeDtypeStruct((RESID, splats), F32),
            jax.ShapeDtypeStruct((COEF, GWORDS), F32),
        ),
        in_specs=[pl.BlockSpec(memory_space=pltpu.SMEM)] * 2 + [pl.BlockSpec(memory_space=vm)] * 10,
        out_specs=(pl.BlockSpec(memory_space=vm),) * 4,
        scratch_shapes=[
            vm((blocks, 8, BLOCK), BF16),
            vm((blocks, 2, PAIRS_B * BLOCK), BF16),
            vm((n_space, 8, BLOCK), BF16),
            vm((n_space, 2, PAIRS_B * BLOCK), BF16),
            vm((n_space, 8, BLOCK), BF16),
            vm((n_space, 2, PAIRS_B * BLOCK), BF16),
            vm((n_code, COEF, GWORDS), BF16),
            vm((pixels, WIDTH), F32),
            vm((pixels, WIDTH), F32),
            vm((pixels, WIDTH), BF16),
            vm((pixels, WIDTH), BF16),
            vm((pixels, WIDTH), F32),
            vm((tiles, GWORDS, WIDTH), BF16),
            vm((tiles, COEF, WIDTH), BF16),
            vm((tiles, COEF, WIDTH), BF16),
            vm((2 * TILE_PIX, WIDTH), BF16),
            vm((2 * TILE_PIX, WIDTH), F32),
            vm((TILE_PIX, WIDTH), BF16),
            vm((WIDTH, WIDTH), BF16),
            vm((WIDTH, WIDTH), BF16),
            vm((16, pixels), F32),
            vm((GROUPS * COEF, GWORDS), F32),
            vm((n_code, COEF, GWORDS), BF16),
            vm((n_code - 1, COEF, GWORDS), BF16),
            vm((n_space, GWORDS), F32),
            vm(((RESID + GEO) * tiles * LIST, BLOCK), F32),
            vm((n_space * STAGE, BLOCK), F32),
            vm((n_space * STAGE, BLOCK), F32),
            vm((n_space, 2, PAIRS_B * BLOCK), BF16),
            vm((n_space, 2, PAIRS_B * BLOCK), BF16),
            vm((n_space, 2, PAIRS_T * BLOCK), BF16),
            vm((n_space, 2, PAIRS_T * BLOCK), BF16),
            vm((blocks * STAGE, BLOCK), F32),
            vm((RESID, splats), F32),
            vm((n_code - 1, RESID, splats // n_code), F32),
            vm((1, 3 * BLOCK), F32),
            vm((n_space // 8, 8, 1, 3 * BLOCK), F32),
            dma((8,)),
            dma((4 * (n_code - 1),)),
            dma((4 * (n_code - 1),)),
            dma((7,)),
            dma((7,)),
            dma((n_space // 8 - 1,)),
            dma((n_space // 8 - 1,)),
        ],
        compiler_params=pltpu.CompilerParams(
            collective_id=0, has_side_effects=True, vmem_limit_bytes=56 * 2**20
        ),
        name="step",
    )(
        sent,
        tile_list[0],
        sent.reshape(1, n_space),
        tile_list.reshape(1, tiles * LIST),
        geometry[0],
        word_ids.reshape(blocks, BLOCK),
        residual,
        codebook,
        rays[0],
        target[0],
        perm,
        spread,
    )
    return (image[None], foot[None], resid_grad, code_grad)


def solution(mesh):
    placed = (
        P("code", None, "space"),
        P(None, "code"),
        P("space"),
        P(None, "space"),
        P("code", "space", None),
        P("code", "space", None),
        P("code", None, "space"),
        P("code", None, "space"),
    )
    return jax.shard_map(
        on_device,
        mesh=mesh,
        in_specs=placed,
        out_specs=(
            P("code", None, "space"),
            P("code", None, "space"),
            P(None, "space"),
            P(None, "code"),
        ),
        check_vma=False,
    )
```

time: 273 us -> 130 us (0.48)
  blocking collectives: 171 us -> 0 us
  Pallas kernels: 24.1 us -> 120 us
  waiting for transfers between devices: 31.5 us -> 0 us
  starting transfers between devices: 24.8 us -> 0 us
  between operations: 14.1 us -> 0.66 us
  local copies, waits for them, and re-layouts: 6.01 us -> 9.14 us
    all_gather x2 -> x0, blocking collectives: 110 us -> none  [the longest x1 98.2 us: on_device(): code = lax.all_gather(word_sum, 'space', axis=0).reshape(16, 8, 3, BLOCK)]
    pallas_call x3 -> x1, Pallas kernels: 24.1 us -> 120 us  [on_device(): pl.pallas_call(functools.partial(step_kernel, n_space, n_code), out_shape...]
    all_to_all x1 -> x0, blocking collectives: 61.2 us -> none  [on_device(): lax.all_to_all(back, 'space', split_axis=0, concat_axis=0, tiled=True)]
    all_to_all x2 -> x0, waiting for transfers between devices: 31.5 us -> none  [the longest x1 29.8 us: on_device(): lax.all_to_all(message, 'space', split_axis=0, concat_axis=0, tiled=True)]
    all_to_all x2 -> x0, starting transfers between devices: 24.7 us -> none  [the longest x1 20.7 us: on_device(): lax.all_to_all(message, 'space', split_axis=0, concat_axis=0, tiled=True)]
    unnamed x18 -> x15, local copies, waits for them, and re-layouts: 3.24 us -> 7.2 us
  transfers between devices with their start and end apart: 3 -> 0, of which waited for: 2 -> 0; matrix products, arithmetic and copies ran while one was open for 1% -> 0% of each run, Pallas kernels for 0% -> 0%
where the time goes in v2:
time: 130 us; the launch traced here: 129 us
  Pallas kernels  120 us (92%)
  local copies, waits for them, and re-layouts  9.14 us (7%)
    pallas_call x1, Pallas kernels, on_device(): pl.pallas_call(functools.partial(step_kernel, n_space, n_code), out_shape...  120 us
    unnamed x15, local copies, waits for them, and re-layouts  7.2 us

profile of v2, /device:TPU:1, one launch (start us, length us, event | category | flops | bytes accessed | tf_op | source)
XLA Modules:
  0.0 129.3 jit_solution(6720742886450067683)
XLA Ops:
  0.6 0.0 copy-start.2
  0.6 1.4 %copy.19.tile_ref = s32[8,4]{1,0:T(8,128)} copy(s32[8,4]{0,1:T(4,128)} %bitcast.19) | data formatting | bytes 256 | tf_op jit(solution)/shard_map/squeeze | solution.py:687
  2.0 0.8 copy.18
  2.7 0.6 reshape.14.tile_row_ref
  3.3 0.0 copy-done.2
  3.3 0.0 copy-start.3
  3.3 0.6 copy.27
  4.0 0.1 copy-done.3
  4.1 0.6 copy.26
  4.7 119.5 %step.1 = (f32[3,2048]{1,0:T(4,128)}, f32[6,8192]{1,0:T(8,128)}, f32[12,8192]{1,0:T(8,128)}, f32[48,1024]{1,0:T(8,128)}) custom-call(s32[128]{0:T(128)} %bitcast.20, s32[8,4]{1,0:T(8,128)} %copy.19.tile_ref, s32[1,128]{1,0:T(1,128)} %bitcast.21, s32[1,32]{1,0:T(1,128)} %reshape.14.tile_row_ref, bf16[6,8192]{1,0:T(8,128)(2,1)} %bitcast.16, ...), custom_call_target="tpu_custom_call" | custom-call | tf_op jit(solution)/shard_map/step/pallas_call | solution.py:625
  124.2 0.0 copy-start
  124.2 1.4 %copy.20 = f32[1,3,2048]{2,0,1:T(1,128)} copy(f32[1,3,2048]{2,1,0:T(4,128)} %bitcast.18) | data formatting | bytes 49152
  125.7 1.8 %copy.21 = f32[1,6,8192]{2,0,1:T(1,128)} copy(f32[1,6,8192]{2,1,0:T(8,128)} %bitcast.13) | data formatting | bytes 393216
  127.5 0.0 copy-done
  127.5 0.0 copy-start.1
  127.5 0.8 copy.30
  128.3 0.3 copy-done.1
  128.6 0.7 copy.31
Async XLA Ops:
  0.6 2.7 %copy-start.2 = (f32[1,3,2048]{2,0,1:T(1,128)S(1)}, f32[1,3,2048]{2,0,1:T(1,128)}, u32[]{:S(2)}) copy-start(f32[1,3,2048]{2,0,1:T(1,128)} %param.16) | copy-start | bytes 73732
  3.3 0.7 copy-start.3
  124.2 3.3 %copy-start = (f32[12,8192]{1,0:T(8,128)S(1)}, f32[12,8192]{1,0:T(8,128)}, u32[]{:S(2)}) copy-start(f32[12,8192]{1,0:T(8,128)} %get-tuple-element.26) | copy-start | bytes 1179652
  127.5 1.1 copy-start.1

commit v3 on v2

--- a/solution.py
+++ b/solution.py
@@ -20,7 +20,7 @@
 GROUPS = 4
 GWORDS = WORDS // GROUPS
 PAIRS_B = RESID // 2
-PAIRS_T = 5
+PAIRS_T = GEO // 2
 STAGE = 16
 LOG2E = 1.4426950408889634
 F32 = jnp.float32
@@ -90,12 +90,17 @@
     barrier = pltpu.get_barrier_semaphore()
 
     def hello(k, carry):
-        pl.semaphore_signal(
-            barrier, inc=1, device_id={"space": lax.rem(me + k, n_space)}, device_id_type=MESH
-        )
-        return carry
-
-    lax.fori_loop(1, n_space, hello, 0)
+        for d in (lax.rem(me + k, n_space), lax.rem(me + n_space - k, n_space)):
+            pl.semaphore_signal(barrier, inc=1, device_id={"space": d}, device_id_type=MESH)
+        return carry
+
+    lax.fori_loop(1, n_space // 2, hello, 0, unroll=3)
+    pl.semaphore_signal(
+        barrier,
+        inc=1,
+        device_id={"space": lax.rem(me + n_space // 2, n_space)},
+        device_id_type=MESH,
+    )
     for k in range(1, n_code):
         pl.semaphore_signal(
             barrier, inc=1, device_id={"code": lax.rem(x + k, n_code)}, device_id_type=MESH
@@ -123,7 +128,7 @@
         one(lax.rem(me + n_space - k, n_space))
         return carry
 
-    lax.fori_loop(1, n_space // 2, pair, 0)
+    lax.fori_loop(1, n_space // 2, pair, 0, unroll=3)
     one(lax.rem(me + n_space // 2, n_space))
 
 
@@ -165,7 +170,6 @@
     send_ref,
     tile_ref,
     send_row_ref,
-    tile_row_ref,
     geo_ref,
     word_ref,
     resid_ref,
@@ -213,8 +217,10 @@
     own_ref,
     own_resid_ref,
     part_ref,
-    line_ref,
-    lines_ref,
+    lines_out,
+    lines_in,
+    near_ref,
+    code_lines,
     sems,
     code_send,
     code_recv,
@@ -224,7 +230,7 @@
     far_recv,
 ):
     me, x = lax.axis_index("space"), lax.axis_index("code")
-    tiles = tile_ref.shape[0]
+    tiles = tile_ref.shape[1]
     slots = tiles * LIST
     blocks = blocks_a.shape[0]
     half = WIDTH // 2
@@ -239,10 +245,6 @@
         low = (ids & 255).astype(F32)
         geo = geo_ref[:, lanes_of(b)].astype(F32)
         blocks_a[b] = jnp.concatenate([geo, high, low], axis=0).astype(BF16)
-        resid = resid_ref[:, lanes_of(b)].astype(F32)
-        blocks_b[b] = jnp.concatenate(
-            [resid[2 * i : 2 * i + 2] for i in range(PAIRS_B)], axis=1
-        ).astype(BF16)
         return carry
 
     lax.fori_loop(0, blocks, build, 0, unroll=4)
@@ -279,6 +281,14 @@
         msg_b[d] = blocks_b[send_ref[d]]
 
     to_space(n_space, fill_a, msg_a, recv_a, sems.at[0], sems.at[1])
+    def build_b(b, carry):
+        resid = resid_ref[:, lanes_of(b)].astype(F32)
+        blocks_b[b] = jnp.concatenate(
+            [resid[2 * i : 2 * i + 2] for i in range(PAIRS_B)], axis=1
+        ).astype(BF16)
+        return carry
+
+    lax.fori_loop(0, blocks, build_b, 0, unroll=4)
     to_space(n_space, fill_b, msg_b, recv_b, sems.at[2], sems.at[3])
     recv_a[me] = blocks_a[send_ref[me]]
     recv_b[me] = blocks_b[send_ref[me]]
@@ -287,13 +297,13 @@
     col_i = lax.broadcasted_iota(jnp.int32, (WIDTH, WIDTH), 1)
     tri_ref[...] = jnp.where(row_i < col_i, 1.0, 0.0).astype(BF16)
     tris_ref[...] = jnp.where(row_i > col_i, 1.0, 0.0).astype(BF16)
-    for j, row in enumerate(harmonic_rows(rays_ref[0:1, :], rays_ref[1:2, :], rays_ref[2:3, :])):
+    for j, row in enumerate(harmonic_rows(rays_ref[0], rays_ref[1], rays_ref[2])):
         harm_ref[j : j + 1, :] = row
     words_ref[...] = jnp.zeros_like(words_ref)
     u = lax.broadcasted_iota(jnp.int32, (SIDE, WIDTH), 0).astype(F32) - (SIDE - 1) * 0.5
 
     def message(t):
-        return jnp.concatenate([recv_a[tile_ref[t, l]] for l in range(LIST)], axis=1).astype(F32)
+        return jnp.concatenate([recv_a[tile_ref[l, t]] for l in range(LIST)], axis=1).astype(F32)
 
     def v_rows(t, v):
         return pl.ds(pl.multiple_of(t * TILE_PIX + v * SIDE, SIDE), SIDE)
@@ -355,7 +365,7 @@
 
     def color_step(t, carry):
         pix = lanes_of(t, TILE_PIX)
-        resid = jnp.concatenate([unpair(recv_b, tile_ref[t, l]) for l in range(LIST)], axis=1)
+        resid = jnp.concatenate([unpair(recv_b, tile_ref[l, t]) for l in range(LIST)], axis=1)
         looked = look_ref[t].astype(F32)
         eight = lax.broadcasted_iota(jnp.int32, (8, WIDTH), 0)
         palette = jnp.concatenate(
@@ -366,48 +376,49 @@
         weight_lo = wl_ref[pix, :]
         mixed = nt(palette, weight) + nt(palette, weight_lo)
         harm = harm_ref[:, pix]
-        image = jnp.concatenate(
-            [
-                jnp.sum(harm * mixed[ch * 16 : (ch + 1) * 16], axis=0, keepdims=True)
-                + mixed[48:49]
-                for ch in range(3)
-            ],
-            axis=0,
-        )
-        img_ref[:, pix] = image
-        off = image - target_ref[:, pix].astype(F32) / 255.0
-        total = off[0:1] + off[1:2] + off[2:3]
+        image = [
+            jnp.sum(harm * mixed[ch * 16 : (ch + 1) * 16], axis=0, keepdims=True) + mixed[48:49]
+            for ch in range(3)
+        ]
+        for ch in range(3):
+            img_ref[ch, :, pix] = image[ch]
+        off = [image[ch] - target_ref[ch, :, pix].astype(F32) / 255.0 for ch in range(3)]
+        total = off[0] + off[1] + off[2]
         pix8 = lax.broadcasted_iota(jnp.int32, (8, TILE_PIX), 0)
         grad = jnp.concatenate(
-            [harm * off[ch : ch + 1] for ch in range(3)] + [jnp.where(pix8 == 0, total, 0.0)],
+            [harm * off[ch] for ch in range(3)] + [jnp.where(pix8 == 0, total, 0.0)],
             axis=0,
         )
         grad_hi = grad.astype(BF16)
         grad_lo = (grad - grad_hi.astype(F32)).astype(BF16)
-        g_ref[pix, :] = tn(grad_hi, palette) + tn(grad_lo, palette)
-        color = nn(grad_hi, weight) + nn(grad_lo, weight) + nn(grad_hi, weight_lo)
+        both = jnp.concatenate([grad_hi, grad_lo], axis=0)
+        g_ref[pix, :] = tn(both, jnp.concatenate([palette, palette], axis=0))
+        color = nn(both, weight)
+        color = color[:56] + color[56:] + nn(grad_hi, weight_lo)
         natural_ref[t] = tn(perm_ref[...], color.astype(BF16))[:COEF].astype(BF16)
         for j in range(4):
             for ch in range(3):
                 row = color[ch * 16 + j : ch * 16 + j + 1]
                 for l in range(LIST):
-                    grads_ref[pl.ds((3 * j + ch) * slots + t * LIST + l, 1), :] = row[
+                    grads_ref[pl.ds((3 * j + ch) * slots + l * tiles + t, 1), :] = row[
                         :, l * BLOCK : (l + 1) * BLOCK
                     ]
         return carry
 
     every_b = finish(msg_b, recv_b, 2)
-    lax.fori_loop(0, tiles, color_step, 0)
-
-    slot_d = lax.broadcasted_iota(jnp.int32, (n_space, slots), 0)
-    slot_hot = jnp.where(slot_d == tile_row_ref[...], 1.0, 0.0)
-    slot_hot = jnp.concatenate([slot_hot, slot_hot], axis=1).astype(BF16)
+    lax.fori_loop(0, tiles, color_step, 0, unroll=2)
+
+    lane_d = lax.broadcasted_iota(jnp.int32, (1, n_space), 1)
+    slot_hot = [
+        jnp.where(lane_d == tile_ref[l, t], 1.0, 0.0) for l in range(LIST) for t in range(tiles)
+    ]
+    slot_hot = jnp.concatenate(slot_hot * 2, axis=0).astype(BF16)
 
     def to_slots(r, ref, row):
         part = grads_ref[r * slots : (r + 1) * slots, :]
         part_hi = part.astype(BF16).astype(F32)
         both = jnp.concatenate([part_hi, part - part_hi], axis=0).astype(BF16)
-        put_rows(ref, row, nn(slot_hot, both))
+        put_rows(ref, row, tn(slot_hot, both))
 
     for r in range(RESID):
         to_slots(r, stage_ref, r)
@@ -477,26 +488,48 @@
         ]
         for r, row in enumerate(rows_back):
             for l in range(LIST):
-                grads_ref[pl.ds((RESID + r) * slots + t * LIST + l, 1), :] = row[
+                grads_ref[pl.ds((RESID + r) * slots + l * tiles + t, 1), :] = row[
                     :, l * BLOCK : (l + 1) * BLOCK
                 ]
         return carry
 
     lax.fori_loop(0, tiles, foot_step, 0)
-    for r in range(GEO):
-        to_slots(RESID + r, stage_t_ref, 4 + r)
     for copy in word_copies:
         copy.wait()
     total = words_ref[pl.ds(pl.multiple_of(x * COEF, COEF), COEF), :]
     for k in range(n_code - 1):
         total = total + theirs_ref[k].astype(F32)
     wide_ref[...] = nn(spread_ref[...], total.astype(BF16))
-    row8 = lax.broadcasted_iota(jnp.int32, (8, BLOCK), 0)
+    planes, crowd = n_space // 8, 8
+    plane, place = me // crowd, lax.rem(me, crowd)
+    for j in range(planes):
+        third = wide_ref[8 * j + 2 : 8 * j + 3, :]
+        third = jnp.concatenate([third[:, : GWORDS // 2], third[:, GWORDS // 2 :]], axis=0)
+        lines_out[j] = jnp.concatenate([wide_ref[8 * j : 8 * j + 2, :], third], axis=1).astype(BF16)
+
+    def along(src, dst, first):
+        copies = []
+        for k in range(1, planes):
+            there = lax.rem(plane + k, planes)
+            copies.append(
+                pltpu.make_async_remote_copy(
+                    src_ref=src(there),
+                    dst_ref=dst,
+                    send_sem=far_send.at[first + k - 1],
+                    recv_sem=far_recv.at[first + k - 1],
+                    device_id={"space": there * crowd + place},
+                    device_id_type=MESH,
+                )
+            )
+            copies[-1].start()
+        return copies
+
+    line_copies = along(lambda there: lines_out.at[there], lines_in.at[plane], 0)
+    lines_in[plane] = lines_out[plane]
+    for r in range(GEO):
+        to_slots(RESID + r, stage_t_ref, r)
 
     def fill_t(d):
-        own = pl.ds(pl.multiple_of(d * STAGE, STAGE), 8)
-        word = wide_ref[pl.ds(pl.multiple_of(d // 8 * 8, 8), 8), lanes_of(lax.rem(d, 8))]
-        stage_t_ref[own, :] = jnp.where(row8 < 4, word, stage_t_ref[own, :])
         for i in range(PAIRS_T):
             msg_t[d, :, i * BLOCK : (i + 1) * BLOCK] = stage_t_ref[
                 pl.ds(pl.multiple_of(d * STAGE, STAGE) + 2 * i, 2), :
@@ -506,9 +539,28 @@
     fill_t(me)
     recv_t[me] = msg_t[me]
 
-    own_b = lax.broadcasted_iota(jnp.int32, (blocks + 8, n_space), 0)
-    own_hot = jnp.where(own_b == send_row_ref[...], 1.0, 0.0)
-    own_hot = jnp.where(own_b == blocks, 1.0, own_hot).astype(BF16)
+    for copy in line_copies:
+        copy.wait()
+    total = lines_in[0].astype(F32)
+    for j in range(1, planes):
+        total = total + lines_in[j].astype(F32)
+    near_ref[place] = total
+    near = []
+    for k in range(1, crowd):
+        near.append(
+            pltpu.make_async_remote_copy(
+                src_ref=near_ref.at[place],
+                dst_ref=near_ref.at[place],
+                send_sem=near_send.at[k - 1],
+                recv_sem=near_recv.at[k - 1],
+                device_id={"space": plane * crowd + lax.rem(place + k, crowd)},
+                device_id_type=MESH,
+            )
+        )
+        near[-1].start()
+
+    own_b = lax.broadcasted_iota(jnp.int32, (blocks, n_space), 0)
+    own_hot = jnp.where(own_b == send_row_ref[...], 1.0, 0.0).astype(BF16)
 
     def spread_pairs(ref, stage, pairs):
         def one(d, carry):
@@ -526,7 +578,7 @@
     every_r = finish(msg_r, recv_r, 4)
     spread_pairs(recv_r, stage_ref, PAIRS_B)
     for r in range(RESID):
-        put_rows(own_ref, r, owned(stage_ref, r)[:blocks])
+        put_rows(own_ref, r, owned(stage_ref, r))
 
     def write_resid(b, carry):
         own_resid_ref[:, lanes_of(b)] = own_ref[pl.ds(pl.multiple_of(b * STAGE, STAGE), STAGE), :][
@@ -541,6 +593,13 @@
         lambda k: part_ref.at[k - 1],
         6,
     )
+    for copy in near:
+        copy.wait()
+    total = near_ref[0]
+    for k in range(1, crowd):
+        total = total + near_ref[k]
+    code_lines[plane] = total.astype(BF16)
+    far = along(lambda there: code_lines.at[plane], code_lines.at[plane], planes - 1)
     for copy in resid_copies:
         copy.wait()
     total = own_resid_ref[:, lanes_of(x, width)]
@@ -555,56 +614,15 @@
 
     every_t = finish(msg_t, recv_t, 6)
     spread_pairs(recv_t, stage_t_ref, PAIRS_T)
-    line_ref[...] = jnp.concatenate(
-        [owned(stage_t_ref, r)[blocks : blocks + 1] for r in range(3)], axis=1
-    )
-    plane, place = me // 8, lax.rem(me, 8)
-    lines_ref[plane, place] = line_ref[...]
-    near = []
-    for k in range(1, 8):
-        near.append(
-            pltpu.make_async_remote_copy(
-                src_ref=line_ref,
-                dst_ref=lines_ref.at[plane, place],
-                send_sem=near_send.at[k - 1],
-                recv_sem=near_recv.at[k - 1],
-                device_id={"space": plane * 8 + lax.rem(place + k, 8)},
-                device_id_type=MESH,
-            )
-        )
-        near[-1].start()
-    for copy in near:
-        copy.wait()
-    planes = n_space // 8
-    far = []
-    for k in range(1, planes):
-        far.append(
-            pltpu.make_async_remote_copy(
-                src_ref=lines_ref.at[plane],
-                dst_ref=lines_ref.at[plane],
-                send_sem=far_send.at[k - 1],
-                recv_sem=far_recv.at[k - 1],
-                device_id={"space": lax.rem(plane + k, planes) * 8 + place},
-                device_id_type=MESH,
-            )
-        )
-        far[-1].start()
     for r in range(GEO):
-        put_rows(own_ref, r, owned(stage_t_ref, 4 + r)[:blocks])
-
-    def write_foot(b, carry):
-        foot_ref[:, lanes_of(b)] = own_ref[pl.ds(pl.multiple_of(b * STAGE, STAGE), 8), :][:GEO]
-        return carry
-
-    lax.fori_loop(0, blocks, write_foot, 0, unroll=4)
+        foot_ref[r] = owned(stage_t_ref, r)
     for copy in far:
         copy.wait()
-    for d in range(n_space):
-        for i in range(3):
-            row = d // 8 * 3 + i
-            code_out_ref[row : row + 1, d % 8 * BLOCK : (d % 8 + 1) * BLOCK] = lines_ref[
-                d // 8, d % 8, :, i * BLOCK : (i + 1) * BLOCK
-            ]
+    for j in range(planes):
+        rows = code_lines[j].astype(F32)
+        code_out_ref[3 * j : 3 * j + 2, :] = rows[:, :GWORDS]
+        code_out_ref[3 * j + 2 : 3 * j + 3, : GWORDS // 2] = rows[0:1, GWORDS:]
+        code_out_ref[3 * j + 2 : 3 * j + 3, GWORDS // 2 :] = rows[1:2, GWORDS:]
     for copy in resid_copies:
         copy.wait()
     for every in (every_a, every_b, every_r, every_t):
@@ -625,12 +643,12 @@
     image, foot, resid_grad, code_grad = pl.pallas_call(
         functools.partial(step_kernel, n_space, n_code),
         out_shape=(
-            jax.ShapeDtypeStruct((3, pixels), F32),
-            jax.ShapeDtypeStruct((GEO, splats), F32),
+            jax.ShapeDtypeStruct((3, 1, pixels), F32),
+            jax.ShapeDtypeStruct((GEO, blocks, BLOCK), F32),
             jax.ShapeDtypeStruct((RESID, splats), F32),
             jax.ShapeDtypeStruct((COEF, GWORDS), F32),
         ),
-        in_specs=[pl.BlockSpec(memory_space=pltpu.SMEM)] * 2 + [pl.BlockSpec(memory_space=vm)] * 10,
+        in_specs=[pl.BlockSpec(memory_space=pltpu.SMEM)] * 2 + [pl.BlockSpec(memory_space=vm)] * 9,
         out_specs=(pl.BlockSpec(memory_space=vm),) * 4,
         scratch_shapes=[
             vm((blocks, 8, BLOCK), BF16),
@@ -668,15 +686,17 @@
             vm((blocks * STAGE, BLOCK), F32),
             vm((RESID, splats), F32),
             vm((n_code - 1, RESID, splats // n_code), F32),
-            vm((1, 3 * BLOCK), F32),
-            vm((n_space // 8, 8, 1, 3 * BLOCK), F32),
+            vm((n_space // 8, 2, 3 * GWORDS // 2), BF16),
+            vm((n_space // 8, 2, 3 * GWORDS // 2), BF16),
+            vm((8, 2, 3 * GWORDS // 2), F32),
+            vm((n_space // 8, 2, 3 * GWORDS // 2), BF16),
             dma((8,)),
             dma((4 * (n_code - 1),)),
             dma((4 * (n_code - 1),)),
             dma((7,)),
             dma((7,)),
-            dma((n_space // 8 - 1,)),
-            dma((n_space // 8 - 1,)),
+            dma((2 * (n_space // 8 - 1),)),
+            dma((2 * (n_space // 8 - 1),)),
         ],
         compiler_params=pltpu.CompilerParams(
             collective_id=0, has_side_effects=True, vmem_limit_bytes=56 * 2**20
@@ -684,19 +704,20 @@
         name="step",
     )(
         sent,
-        tile_list[0],
+        tile_list[0].T,
         sent.reshape(1, n_space),
-        tile_list.reshape(1, tiles * LIST),
         geometry[0],
         word_ids.reshape(blocks, BLOCK),
         residual,
         codebook,
-        rays[0],
-        target[0],
+        jnp.swapaxes(rays, 0, 1),
+        jnp.swapaxes(target, 0, 1),
         perm,
         spread,
     )
-    return (image[None], foot[None], resid_grad, code_grad)
+    image = jnp.swapaxes(image, 0, 1)
+    foot = jnp.swapaxes(foot.reshape(GEO, 1, splats), 0, 1)
+    return (image, foot, resid_grad, code_grad)
 
 
 def solution(mesh):

time: 130 us -> 114 us (0.88)
  the two profiles are of different devices: /device:TPU:1 before, /device:TPU:32 now
where the time goes in v3:
time: 114 us
  Pallas kernels  108 us (95%)
  local copies, waits for them, and re-layouts  5.55 us (5%)
    pallas_call x1, Pallas kernels, on_device(): pl.pallas_call(functools.partial(step_kernel, n_space, n_code), out_shape...  108 us
    unnamed x6, local copies, waits for them, and re-layouts  5.55 us

profile of v3, /device:TPU:32, one launch (start us, length us, event | category | flops | bytes accessed | tf_op | source)
XLA Modules:
  0.0 114.1 jit_solution(1579027871100533128)
XLA Ops:
  0.6 107.9 %step.1 = (f32[3,1,2048]{2,1,0:T(1,128)}, f32[6,64,128]{2,1,0:T(8,128)}, f32[12,8192]{1,0:T(8,128)}, f32[48,1024]{1,0:T(8,128)}) custom-call(s32[128]{0:T(128)} %bitcast.18, s32[4,8]{1,0:T(4,128)} %bitcast.17, s32[1,128]{1,0:T(1,128)} %bitcast.19, bf16[6,8192]{1,0:T(8,128)(2,1)} %bitcast.12, s32[64,128]{1,0:T(8,128)} %bitcast.13, ...), custom_call_target="tpu_custom_call" | custom-call | tf_op jit(solution)/shard_map/step/pallas_call | solution.py:643
  108.6 1.3 %copy.20 = f32[1,3,2048]{2,0,1:T(1,128)} copy(f32[1,3,2048]{2,0,1:T(1,128)} %bitcast.16) | data formatting | bytes 49152
  109.9 1.6 %copy.21 = f32[1,6,8192]{2,0,1:T(1,128)} copy(f32[1,6,8192]{2,0,1:T(1,128)} %bitcast.11) | data formatting | bytes 393216
  111.5 0.0 copy-start
  111.5 1.9 %copy.22 = f32[12,8192]{1,0:T(8,128)} copy(f32[12,8192]{1,0:T(8,128)} %get-tuple-element.26) | data formatting | bytes 786432
  113.4 0.0 copy-done
  113.4 0.7 copy.23
Async XLA Ops:
  111.5 1.9 %copy-start = (f32[48,1024]{1,0:T(8,128)S(1)}, f32[48,1024]{1,0:T(8,128)}, u32[]{:S(2)}) copy-start(f32[48,1024]{1,0:T(8,128)} %get-tuple-element.27) | copy-start | bytes 589828

commit v4 on v3

--- a/solution.py
+++ b/solution.py
@@ -108,7 +108,7 @@
     return barrier
 
 
-def to_space(n_space, fill, src, dst, send_sem, recv_sem):
+def to_space(n_space, fill, src, dst, send_sem, recv_sem, first=1, stop=None):
     me = lax.axis_index("space")
 
     def one(d):
@@ -128,8 +128,9 @@
         one(lax.rem(me + n_space - k, n_space))
         return carry
 
-    lax.fori_loop(1, n_space // 2, pair, 0, unroll=3)
-    one(lax.rem(me + n_space // 2, n_space))
+    lax.fori_loop(first, stop or n_space // 2, pair, 0, unroll=3)
+    if stop is None:
+        one(lax.rem(me + n_space // 2, n_space))
 
 
 def all_of(n_space, src, dst, send_sem, recv_sem):
@@ -202,6 +203,7 @@
     wg_ref,
     tri_ref,
     tris_ref,
+    spot_ref,
     harm_ref,
     words_ref,
     mine_ref,
@@ -214,9 +216,9 @@
     recv_r,
     msg_t,
     recv_t,
-    own_ref,
     own_resid_ref,
     part_ref,
+    sum_ref,
     lines_out,
     lines_in,
     near_ref,
@@ -405,20 +407,19 @@
                     ]
         return carry
 
-    every_b = finish(msg_b, recv_b, 2)
-    lax.fori_loop(0, tiles, color_step, 0, unroll=2)
-
     lane_d = lax.broadcasted_iota(jnp.int32, (1, n_space), 1)
     slot_hot = [
         jnp.where(lane_d == tile_ref[l, t], 1.0, 0.0) for l in range(LIST) for t in range(tiles)
     ]
-    slot_hot = jnp.concatenate(slot_hot * 2, axis=0).astype(BF16)
+    spot_ref[...] = jnp.concatenate(slot_hot * (n_space // slots), axis=0).T.astype(BF16)
+    every_b = finish(msg_b, recv_b, 2)
+    lax.fori_loop(0, tiles, color_step, 0, unroll=4)
 
     def to_slots(r, ref, row):
         part = grads_ref[r * slots : (r + 1) * slots, :]
         part_hi = part.astype(BF16).astype(F32)
         both = jnp.concatenate([part_hi, part - part_hi], axis=0).astype(BF16)
-        put_rows(ref, row, tn(slot_hot, both))
+        put_rows(ref, row, nn(spot_ref[:, : 2 * slots], both))
 
     for r in range(RESID):
         to_slots(r, stage_ref, r)
@@ -535,10 +536,42 @@
                 pl.ds(pl.multiple_of(d * STAGE, STAGE) + 2 * i, 2), :
             ].astype(BF16)
 
-    to_space(n_space, fill_t, msg_t, recv_t, sems.at[6], sems.at[7])
-    fill_t(me)
-    recv_t[me] = msg_t[me]
-
+    own_b = lax.broadcasted_iota(jnp.int32, (blocks, n_space), 0)
+    own_hot = jnp.where(own_b == send_row_ref[...], 1.0, 0.0).astype(BF16)
+
+    def spread_pairs(ref, stage, pairs):
+        def one(d, carry):
+            for i in range(pairs):
+                stage[pl.ds(pl.multiple_of(d * STAGE, STAGE) + 2 * i, 2), :] = ref[
+                    d, :, i * BLOCK : (i + 1) * BLOCK
+                ].astype(F32)
+            return carry
+
+        lax.fori_loop(0, n_space, one, 0, unroll=4)
+
+    def owned(stage, row):
+        return nn(own_hot, get_rows(stage, row, n_space).astype(BF16))
+
+    every_r = finish(msg_r, recv_r, 4)
+    spread_pairs(recv_r, stage_ref, PAIRS_B)
+    share = blocks // n_code
+    chunk = RESID * share
+
+    def chunk_of(i):
+        return pl.ds(pl.multiple_of(i * chunk, chunk), chunk)
+
+    for r in range(RESID):
+        own = owned(stage_ref, r)
+        for c in range(n_code):
+            at = c * chunk + r * share
+            own_resid_ref[at : at + share, :] = own[c * share : (c + 1) * share]
+    resid_copies = around(
+        lambda k: own_resid_ref.at[chunk_of(lax.rem(x + k, n_code))],
+        lambda k: part_ref.at[k - 1],
+        6,
+    )
+    middle = n_space // 4 - 1
+    to_space(n_space, fill_t, msg_t, recv_t, sems.at[6], sems.at[7], 1, middle)
     for copy in line_copies:
         copy.wait()
     total = lines_in[0].astype(F32)
@@ -559,40 +592,20 @@
         )
         near[-1].start()
 
-    own_b = lax.broadcasted_iota(jnp.int32, (blocks, n_space), 0)
-    own_hot = jnp.where(own_b == send_row_ref[...], 1.0, 0.0).astype(BF16)
-
-    def spread_pairs(ref, stage, pairs):
-        def one(d, carry):
-            for i in range(pairs):
-                stage[pl.ds(pl.multiple_of(d * STAGE, STAGE) + 2 * i, 2), :] = ref[
-                    d, :, i * BLOCK : (i + 1) * BLOCK
-                ].astype(F32)
-            return carry
-
-        lax.fori_loop(0, n_space, one, 0, unroll=4)
-
-    def owned(stage, row):
-        return nn(own_hot, get_rows(stage, row, n_space).astype(BF16))
-
-    every_r = finish(msg_r, recv_r, 4)
-    spread_pairs(recv_r, stage_ref, PAIRS_B)
-    for r in range(RESID):
-        put_rows(own_ref, r, owned(stage_ref, r))
-
-    def write_resid(b, carry):
-        own_resid_ref[:, lanes_of(b)] = own_ref[pl.ds(pl.multiple_of(b * STAGE, STAGE), STAGE), :][
-            :RESID
-        ]
-        return carry
-
-    lax.fori_loop(0, blocks, write_resid, 0, unroll=4)
-    width = part_ref.shape[2]
+    for copy in resid_copies:
+        copy.wait()
+    total = own_resid_ref[chunk_of(x), :]
+    for k in range(n_code - 1):
+        total = total + part_ref[k]
+    sum_ref[chunk_of(x), :] = total
     resid_copies = around(
-        lambda k: own_resid_ref.at[:, lanes_of(lax.rem(x + k, n_code), width)],
-        lambda k: part_ref.at[k - 1],
-        6,
+        lambda k: sum_ref.at[chunk_of(x)],
+        lambda k: sum_ref.at[chunk_of(x)],
+        9,
     )
+    to_space(n_space, fill_t, msg_t, recv_t, sems.at[6], sems.at[7], middle)
+    fill_t(me)
+    recv_t[me] = msg_t[me]
     for copy in near:
         copy.wait()
     total = near_ref[0]
@@ -600,17 +613,6 @@
         total = total + near_ref[k]
     code_lines[plane] = total.astype(BF16)
     far = along(lambda there: code_lines.at[plane], code_lines.at[plane], planes - 1)
-    for copy in resid_copies:
-        copy.wait()
-    total = own_resid_ref[:, lanes_of(x, width)]
-    for k in range(n_code - 1):
-        total = total + part_ref[k]
-    resid_out_ref[:, lanes_of(x, width)] = total
-    resid_copies = around(
-        lambda k: resid_out_ref.at[:, lanes_of(x, width)],
-        lambda k: resid_out_ref.at[:, lanes_of(x, width)],
-        9,
-    )
 
     every_t = finish(msg_t, recv_t, 6)
     spread_pairs(recv_t, stage_t_ref, PAIRS_T)
@@ -625,8 +627,34 @@
         code_out_ref[3 * j + 2 : 3 * j + 3, GWORDS // 2 :] = rows[1:2, GWORDS:]
     for copy in resid_copies:
         copy.wait()
+    for b in range(blocks):
+        at = b // share * chunk + b % share
+        resid_out_ref[:, b * BLOCK : (b + 1) * BLOCK] = sum_ref[pl.ds(at, RESID, stride=share), :]
     for every in (every_a, every_b, every_r, every_t):
         every.wait_send()
+
+
+def hand_over_kernel(*refs):
+    sems = refs[-1]
+    count = len(refs) // 2
+    copies = [
+        pltpu.make_async_copy(refs[i], refs[count + i], sems.at[i]) for i in range(count)
+    ]
+    for copy in copies:
+        copy.start()
+    for copy in copies:
+        copy.wait()
+
+
+def hand_over(arrays):
+    return pl.pallas_call(
+        hand_over_kernel,
+        out_shape=tuple(jax.ShapeDtypeStruct(a.shape, a.dtype) for a in arrays),
+        in_specs=[pl.BlockSpec(memory_space=pl.ANY)] * len(arrays),
+        out_specs=(pl.BlockSpec(memory_space=pl.ANY),) * len(arrays),
+        scratch_shapes=[pltpu.SemaphoreType.DMA((len(arrays),))],
+        name="hand_over",
+    )(*arrays)
 
 
 def on_device(geometry, codebook, word_ids, residual, send_list, tile_list, rays, target):
@@ -640,7 +668,7 @@
     sent = send_list[0, 0]
     vm = pltpu.VMEM
     dma = pltpu.SemaphoreType.DMA
-    image, foot, resid_grad, code_grad = pl.pallas_call(
+    results = pl.pallas_call(
         functools.partial(step_kernel, n_space, n_code),
         out_shape=(
             jax.ShapeDtypeStruct((3, 1, pixels), F32),
@@ -671,6 +699,7 @@
             vm((TILE_PIX, WIDTH), BF16),
             vm((WIDTH, WIDTH), BF16),
             vm((WIDTH, WIDTH), BF16),
+            vm((n_space, n_space), BF16),
             vm((16, pixels), F32),
             vm((GROUPS * COEF, GWORDS), F32),
             vm((n_code, COEF, GWORDS), BF16),
@@ -683,9 +712,9 @@
             vm((n_space, 2, PAIRS_B * BLOCK), BF16),
             vm((n_space, 2, PAIRS_T * BLOCK), BF16),
             vm((n_space, 2, PAIRS_T * BLOCK), BF16),
-            vm((blocks * STAGE, BLOCK), F32),
-            vm((RESID, splats), F32),
-            vm((n_code - 1, RESID, splats // n_code), F32),
+            vm((RESID * blocks, BLOCK), F32),
+            vm((n_code - 1, RESID * blocks // n_code, BLOCK), F32),
+            vm((RESID * blocks, BLOCK), F32),
             vm((n_space // 8, 2, 3 * GWORDS // 2), BF16),
             vm((n_space // 8, 2, 3 * GWORDS // 2), BF16),
             vm((8, 2, 3 * GWORDS // 2), F32),
@@ -715,6 +744,7 @@
         perm,
         spread,
     )
+    image, foot, resid_grad, code_grad = hand_over(results)
     image = jnp.swapaxes(image, 0, 1)
     foot = jnp.swapaxes(foot.reshape(GEO, 1, splats), 0, 1)
     return (image, foot, resid_grad, code_grad)

time: 114 us -> 142 us (1.25)
  the two profiles are of different devices: /device:TPU:32 before, /device:TPU:1 now
where the time goes in v4:
time: 142 us; the launch traced here: 141 us
  Pallas kernels  140 us (99%)
    pallas_call x1, Pallas kernels, on_device(): pl.pallas_call(functools.partial(step_kernel, n_space, n_code), out_shape...  110 us
    pallas_call x1, Pallas kernels, hand_over(): pl.pallas_call(hand_over_kernel, out_shape=tuple((jax.ShapeDtypeStruct(a....  29.7 us

profile of v4, /device:TPU:1, one launch (start us, length us, event | category | flops | bytes accessed | tf_op | source)
XLA Modules:
  0.0 140.8 jit_solution(2242927243355136626)
XLA Ops:
  0.6 110.5 %step.1 = (f32[3,1,2048]{2,1,0:T(1,128)}, f32[6,64,128]{2,1,0:T(8,128)}, f32[12,8192]{1,0:T(8,128)}, f32[48,1024]{1,0:T(8,128)}) custom-call(s32[128]{0:T(128)} %bitcast.16, s32[4,8]{1,0:T(4,128)} %bitcast.15, s32[1,128]{1,0:T(1,128)} %bitcast.17, bf16[6,8192]{1,0:T(8,128)(2,1)} %bitcast.11, s32[64,128]{1,0:T(8,128)} %bitcast.12, ...), custom_call_target="tpu_custom_call" | custom-call | tf_op jit(solution)/shard_map/step/pallas_call | solution.py:671
  111.1 29.7 %hand_over.1 = (f32[3,1,2048]{2,1,0:T(1,128)}, f32[6,64,128]{2,1,0:T(8,128)}, f32[12,8192]{1,0:T(8,128)}, f32[48,1024]{1,0:T(8,128)}) custom-call(f32[3,1,2048]{2,1,0:T(1,128)} %get-tuple-element.12.refs_0_, f32[6,64,128]{2,1,0:T(8,128)} %get-tuple-element.13.refs_1_, f32[12,8192]{1,0:T(8,128)} %get-tuple-element.14.refs_2_, ...), custom_call_target="tpu_custom_call" | custom-call | tf_op jit(solution)/shard_map/hand_over/pallas_call | solution.py:650

commit v5 on v3

--- a/solution.py
+++ b/solution.py
@@ -108,7 +108,7 @@
     return barrier
 
 
-def to_space(n_space, fill, src, dst, send_sem, recv_sem):
+def to_space(n_space, fill, src, dst, send_sem, recv_sem, first=1, stop=None):
     me = lax.axis_index("space")
 
     def one(d):
@@ -128,8 +128,9 @@
         one(lax.rem(me + n_space - k, n_space))
         return carry
 
-    lax.fori_loop(1, n_space // 2, pair, 0, unroll=3)
-    one(lax.rem(me + n_space // 2, n_space))
+    lax.fori_loop(first, stop or n_space // 2, pair, 0, unroll=3)
+    if stop is None:
+        one(lax.rem(me + n_space // 2, n_space))
 
 
 def all_of(n_space, src, dst, send_sem, recv_sem):
@@ -196,12 +197,15 @@
     g_ref,
     hot_ref,
     look_ref,
-    natural_ref,
+    color_ref,
+    both_ref,
+    palette_ref,
     log_ref,
     cum_ref,
     wg_ref,
     tri_ref,
     tris_ref,
+    spot_ref,
     harm_ref,
     words_ref,
     mine_ref,
@@ -214,9 +218,9 @@
     recv_r,
     msg_t,
     recv_t,
-    own_ref,
     own_resid_ref,
     part_ref,
+    sum_ref,
     lines_out,
     lines_in,
     near_ref,
@@ -392,10 +396,11 @@
         grad_hi = grad.astype(BF16)
         grad_lo = (grad - grad_hi.astype(F32)).astype(BF16)
         both = jnp.concatenate([grad_hi, grad_lo], axis=0)
-        g_ref[pix, :] = tn(both, jnp.concatenate([palette, palette], axis=0))
+        both_ref[t] = both
+        palette_ref[t] = jnp.concatenate([palette, palette], axis=0)
         color = nn(both, weight)
         color = color[:56] + color[56:] + nn(grad_hi, weight_lo)
-        natural_ref[t] = tn(perm_ref[...], color.astype(BF16))[:COEF].astype(BF16)
+        color_ref[t] = color.astype(BF16)
         for j in range(4):
             for ch in range(3):
                 row = color[ch * 16 + j : ch * 16 + j + 1]
@@ -405,20 +410,19 @@
                     ]
         return carry
 
-    every_b = finish(msg_b, recv_b, 2)
-    lax.fori_loop(0, tiles, color_step, 0, unroll=2)
-
     lane_d = lax.broadcasted_iota(jnp.int32, (1, n_space), 1)
     slot_hot = [
         jnp.where(lane_d == tile_ref[l, t], 1.0, 0.0) for l in range(LIST) for t in range(tiles)
     ]
-    slot_hot = jnp.concatenate(slot_hot * 2, axis=0).astype(BF16)
+    spot_ref[...] = jnp.concatenate(slot_hot * (n_space // slots), axis=0).T.astype(BF16)
+    every_b = finish(msg_b, recv_b, 2)
+    lax.fori_loop(0, tiles, color_step, 0, unroll=2)
 
     def to_slots(r, ref, row):
         part = grads_ref[r * slots : (r + 1) * slots, :]
         part_hi = part.astype(BF16).astype(F32)
         both = jnp.concatenate([part_hi, part - part_hi], axis=0).astype(BF16)
-        put_rows(ref, row, tn(slot_hot, both))
+        put_rows(ref, row, nn(spot_ref[:, : 2 * slots], both))
 
     for r in range(RESID):
         to_slots(r, stage_ref, r)
@@ -435,7 +439,7 @@
 
     def word_step(t, carry):
         group = jnp.floor(message(t)[6:7] * 0.25)
-        natural = natural_ref[t].astype(F32)
+        natural = tn(perm_ref[...], color_ref[t])[:COEF]
         masked = jnp.concatenate(
             [jnp.where(group == float(g), natural, 0.0).astype(BF16) for g in range(GROUPS)], axis=0
         )
@@ -453,9 +457,10 @@
         msg = message(t)
         cu, cv, ca, cb, cc, op = [msg[i : i + 1] for i in range(GEO)]
         du = u - cu
+        g_ref[...] = tn(both_ref[t], palette_ref[t])
         for v in range(SIDE):
             rows = slice(v * SIDE, (v + 1) * SIDE)
-            wg_ref[rows, :] = (wp_ref[v_rows(t, v), :] * g_ref[v_rows(t, v), :] * op).astype(BF16)
+            wg_ref[rows, :] = (wp_ref[v_rows(t, v), :] * g_ref[rows, :] * op).astype(BF16)
         cum_ref[:TILE_PIX, half:] = nn(wg_ref[:, half:], tris_ref[half:, half:])
         cum_ref[:TILE_PIX, :half] = nn(wg_ref[...], tris_ref[:, :half])
         s_zero = jnp.zeros((SIDE, WIDTH), F32)
@@ -464,7 +469,7 @@
         for v in range(SIDE):
             rows = slice(v * SIDE, (v + 1) * SIDE)
             e = e_ref[v_rows(t, v), :]
-            p = wp_ref[v_rows(t, v), :] * g_ref[v_rows(t, v), :] - cum_ref[rows, :] * (
+            p = wp_ref[v_rows(t, v), :] * g_ref[rows, :] - cum_ref[rows, :] * (
                 e / (1.0 - op * e)
             )
             dv = (v - (SIDE - 1) * 0.5) - cv
@@ -538,7 +543,6 @@
     to_space(n_space, fill_t, msg_t, recv_t, sems.at[6], sems.at[7])
     fill_t(me)
     recv_t[me] = msg_t[me]
-
     for copy in line_copies:
         copy.wait()
     total = lines_in[0].astype(F32)
@@ -577,19 +581,19 @@
 
     every_r = finish(msg_r, recv_r, 4)
     spread_pairs(recv_r, stage_ref, PAIRS_B)
+    share = blocks // n_code
+    chunk = RESID * share
+
+    def chunk_of(i):
+        return pl.ds(pl.multiple_of(i * chunk, chunk), chunk)
+
     for r in range(RESID):
-        put_rows(own_ref, r, owned(stage_ref, r))
-
-    def write_resid(b, carry):
-        own_resid_ref[:, lanes_of(b)] = own_ref[pl.ds(pl.multiple_of(b * STAGE, STAGE), STAGE), :][
-            :RESID
-        ]
-        return carry
-
-    lax.fori_loop(0, blocks, write_resid, 0, unroll=4)
-    width = part_ref.shape[2]
+        own = owned(stage_ref, r)
+        for c in range(n_code):
+            at = c * chunk + r * share
+            own_resid_ref[at : at + share, :] = own[c * share : (c + 1) * share]
     resid_copies = around(
-        lambda k: own_resid_ref.at[:, lanes_of(lax.rem(x + k, n_code), width)],
+        lambda k: own_resid_ref.at[chunk_of(lax.rem(x + k, n_code))],
         lambda k: part_ref.at[k - 1],
         6,
     )
@@ -602,13 +606,13 @@
     far = along(lambda there: code_lines.at[plane], code_lines.at[plane], planes - 1)
     for copy in resid_copies:
         copy.wait()
-    total = own_resid_ref[:, lanes_of(x, width)]
+    total = own_resid_ref[chunk_of(x), :]
     for k in range(n_code - 1):
         total = total + part_ref[k]
-    resid_out_ref[:, lanes_of(x, width)] = total
+    sum_ref[chunk_of(x), :] = total
     resid_copies = around(
-        lambda k: resid_out_ref.at[:, lanes_of(x, width)],
-        lambda k: resid_out_ref.at[:, lanes_of(x, width)],
+        lambda k: sum_ref.at[chunk_of(x)],
+        lambda k: sum_ref.at[chunk_of(x)],
         9,
     )
 
@@ -625,8 +629,27 @@
         code_out_ref[3 * j + 2 : 3 * j + 3, GWORDS // 2 :] = rows[1:2, GWORDS:]
     for copy in resid_copies:
         copy.wait()
+    for b in range(blocks):
+        at = b // share * chunk + b % share
+        resid_out_ref[:, b * BLOCK : (b + 1) * BLOCK] = sum_ref[pl.ds(at, RESID, stride=share), :]
     for every in (every_a, every_b, every_r, every_t):
         every.wait_send()
+
+
+def hand_over_kernel(*refs):
+    count = len(refs) // 2
+    for i in range(count):
+        refs[count + i][...] = refs[i][...]
+
+
+def hand_over(arrays):
+    return pl.pallas_call(
+        hand_over_kernel,
+        out_shape=tuple(jax.ShapeDtypeStruct(a.shape, a.dtype) for a in arrays),
+        in_specs=[pl.BlockSpec(memory_space=pltpu.VMEM)] * len(arrays),
+        out_specs=(pl.BlockSpec(memory_space=pltpu.VMEM),) * len(arrays),
+        name="hand_over",
+    )(*arrays)
 
 
 def on_device(geometry, codebook, word_ids, residual, send_list, tile_list, rays, target):
@@ -640,7 +663,7 @@
     sent = send_list[0, 0]
     vm = pltpu.VMEM
     dma = pltpu.SemaphoreType.DMA
-    image, foot, resid_grad, code_grad = pl.pallas_call(
+    results = pl.pallas_call(
         functools.partial(step_kernel, n_space, n_code),
         out_shape=(
             jax.ShapeDtypeStruct((3, 1, pixels), F32),
@@ -662,15 +685,18 @@
             vm((pixels, WIDTH), F32),
             vm((pixels, WIDTH), BF16),
             vm((pixels, WIDTH), BF16),
-            vm((pixels, WIDTH), F32),
+            vm((TILE_PIX, WIDTH), F32),
             vm((tiles, GWORDS, WIDTH), BF16),
             vm((tiles, COEF, WIDTH), BF16),
-            vm((tiles, COEF, WIDTH), BF16),
+            vm((tiles, 56, WIDTH), BF16),
+            vm((tiles, 112, TILE_PIX), BF16),
+            vm((tiles, 112, WIDTH), BF16),
             vm((2 * TILE_PIX, WIDTH), BF16),
             vm((2 * TILE_PIX, WIDTH), F32),
             vm((TILE_PIX, WIDTH), BF16),
             vm((WIDTH, WIDTH), BF16),
             vm((WIDTH, WIDTH), BF16),
+            vm((n_space, n_space), BF16),
             vm((16, pixels), F32),
             vm((GROUPS * COEF, GWORDS), F32),
             vm((n_code, COEF, GWORDS), BF16),
@@ -683,9 +709,9 @@
             vm((n_space, 2, PAIRS_B * BLOCK), BF16),
             vm((n_space, 2, PAIRS_T * BLOCK), BF16),
             vm((n_space, 2, PAIRS_T * BLOCK), BF16),
-            vm((blocks * STAGE, BLOCK), F32),
-            vm((RESID, splats), F32),
-            vm((n_code - 1, RESID, splats // n_code), F32),
+            vm((RESID * blocks, BLOCK), F32),
+            vm((n_code - 1, RESID * blocks // n_code, BLOCK), F32),
+            vm((RESID * blocks, BLOCK), F32),
             vm((n_space // 8, 2, 3 * GWORDS // 2), BF16),
             vm((n_space // 8, 2, 3 * GWORDS // 2), BF16),
             vm((8, 2, 3 * GWORDS // 2), F32),
@@ -715,6 +741,7 @@
         perm,
         spread,
     )
+    image, foot, resid_grad, code_grad = hand_over(results)
     image = jnp.swapaxes(image, 0, 1)
     foot = jnp.swapaxes(foot.reshape(GEO, 1, splats), 0, 1)
     return (image, foot, resid_grad, code_grad)

time: 114 us -> 105 us (0.921)
  the two profiles are of different devices: /device:TPU:32 before, /device:TPU:1 now
where the time goes in v5:
time: 105 us; the launch traced here: 104 us
  Pallas kernels  103 us (98%)
    pallas_call x1, Pallas kernels, on_device(): pl.pallas_call(functools.partial(step_kernel, n_space, n_code), out_shape...  101 us
    pallas_call x1, Pallas kernels, hand_over(): pl.pallas_call(hand_over_kernel, out_shape=tuple((jax.ShapeDtypeStruct(a....  2.15 us

profile of v5, /device:TPU:1, one launch (start us, length us, event | category | flops | bytes accessed | tf_op | source)
XLA Modules:
  0.0 104.1 jit_solution(9916743488760442409)
XLA Ops:
  0.6 101.3 %step.1 = (f32[3,1,2048]{2,1,0:T(1,128)}, f32[6,64,128]{2,1,0:T(8,128)}, f32[12,8192]{1,0:T(8,128)}, f32[48,1024]{1,0:T(8,128)}) custom-call(s32[128]{0:T(128)} %bitcast.16, s32[4,8]{1,0:T(4,128)} %bitcast.15, s32[1,128]{1,0:T(1,128)} %bitcast.17, bf16[6,8192]{1,0:T(8,128)(2,1)} %bitcast.11, s32[64,128]{1,0:T(8,128)} %bitcast.12, ...), custom_call_target="tpu_custom_call" | custom-call | tf_op jit(solution)/shard_map/step/pallas_call | solution.py:666
  101.9 2.1 %hand_over.1 = (f32[3,1,2048]{2,1,0:T(1,128)}, f32[6,64,128]{2,1,0:T(8,128)}, f32[12,8192]{1,0:T(8,128)}, f32[48,1024]{1,0:T(8,128)}) custom-call(f32[3,1,2048]{2,1,0:T(1,128)} %get-tuple-element.12.refs_0_, f32[6,64,128]{2,1,0:T(8,128)} %get-tuple-element.13.refs_1_, f32[12,8192]{1,0:T(8,128)} %get-tuple-element.14.refs_2_, ...), custom_call_target="tpu_custom_call" | custom-call | tf_op jit(solution)/shard_map/hand_over/pallas_call | solution.py:646
